TPU v7x, 512 devices: a whole 4x8x8 slice. The times are simulated.
512 devices in a mesh: seq: 64 (over y, x, z_lo), tensor: 8 (over z_hi, core).
Axes of the slice: x: 4, y: 8, z: 8 (z_hi: 4, z_lo: 2; z = z_hi * 2 + z_lo), core: 2. Of those that a mesh axis runs over, the one named last changes fastest.
Arguments:
- queries: bfloat16 [8192, 3072], P('seq', 'tensor'), may hold values from -12 to 12
- keys: bfloat16 [8192, 3072], P('seq', 'tensor'), may hold values from -6 to 6
- values: bfloat16 [8192, 3072], P('seq', 'tensor'), may hold values from -6 to 6
- residual: bfloat16 [8192, 6144], P('seq', 'tensor'), may hold values from -40 to 40
- out_weight: bfloat16 [3072, 6144], P('seq', 'tensor'), may hold values from -0.109375 to 0.109375
- pred_hidden: bfloat16 [2, 8192, 1024], P(None, 'seq'), may hold values from -16 to 16
- pred_weight: bfloat16 [1024, 6144], P(None, 'tensor'), may hold values from -0.1875 to 0.1875
- mask: int32 [2, 8192], P(None, 'seq'), may hold values from 0 to 1, as said below
Outputs:
- target: bfloat16 [8192, 6144], P('seq', 'tensor')
- pred_grad: float32 [1024, 6144], P('seq', 'tensor')
Inputs may be any that keep to these rules, and one draw needn't show every extreme that they name: In each clip c, each mask marks the same 384 spatial positions s in every time step t, position c * 4096 + t * 512 + s; so it marks 3072 positions of each clip.
All inputs are finite; a program needn't handle non-finite values.
Results may differ from a plain program's by a relative error of at most 0.0035.
Values may be sent and summed in bfloat16 or wider, within the bound.
No kernel may reach another device: no remote copies, remote signals or barrier semaphores. Data moves between devices by JAX's collectives and lax.ppermute only.
A program may use at most 64 MiB of HBM per device.

v0:
```python
import math

import jax
import jax.numpy as jnp
from jax import lax
from jax.sharding import PartitionSpec as P

D = 6144
HD = 128
CLIP = 4096
MASKS = 2
MASKED = 3072


def swapped(value, axis, distance):
    mask = 2**distance
    pairs = [(source, source ^ mask) for source in range(lax.axis_size(axis))]
    return lax.ppermute(value, axis, pairs)


def body(queries, keys, values, residual, out_weight, pred_hidden, pred_weight, mask):
    tokens_here = queries.shape[0]
    local_heads = queries.shape[1] // HD
    query_heads = queries.reshape(tokens_here, local_heads, HD)
    inverse_root = 1.0 / math.sqrt(HD)
    shards = CLIP // tokens_here
    bit_count = shards.bit_length() - 1

    def attend(carry, stacked):
        best, total, accum = carry
        rows_in = stacked.shape[1]
        key_heads = stacked[0].reshape(rows_in, local_heads, HD)
        value_heads = stacked[1].reshape(rows_in, local_heads, HD)
        scores = (
            jnp.einsum("qhd,khd->hqk", query_heads, key_heads, preferred_element_type=jnp.float32)
            * inverse_root
        )
        newbest = jnp.maximum(best, jnp.max(scores, axis=2))
        factor = jnp.exp(best - newbest)
        exponent = jnp.exp(scores - newbest[:, :, None])
        total = total * factor + jnp.sum(exponent, axis=2)
        accum = accum * factor[:, :, None] + jnp.einsum(
            "hqk,khd->hqd",
            exponent.astype(jnp.bfloat16),
            value_heads,
            preferred_element_type=jnp.float32,
        )
        return (newbest, total, accum)

    start_state = (
        jnp.full((local_heads, tokens_here), -1e30, jnp.float32),
        jnp.zeros((local_heads, tokens_here), jnp.float32),
        jnp.zeros((local_heads, tokens_here, HD), jnp.float32),
    )
    held = jnp.stack((keys, values))
    state = attend(start_state, held)
    bit_order = list(range(bit_count))
    for step_number, bit_number in enumerate(bit_order):
        arrived = swapped(held, "seq", bit_number)
        state = attend(state, arrived)
        if step_number + 1 < bit_count:
            held = jnp.concatenate((held, arrived), axis=1)
    best, total, accum = state
    attended = (
        (accum / total[:, :, None])
        .astype(jnp.bfloat16)
        .transpose(1, 0, 2)
        .reshape(tokens_here, local_heads * HD)
    )
    attended_all = lax.all_gather(attended, "tensor", axis=1, tiled=True)
    columns = attended_all
    projected = jnp.dot(
        columns,
        lax.all_gather(out_weight, "seq", axis=0, tiled=True),
        preferred_element_type=jnp.float32,
    )
    summed = residual.astype(jnp.float32) + projected
    mean = lax.psum(jnp.sum(summed, axis=1), "tensor") / D
    centered = summed - mean[:, None]
    var = lax.psum(jnp.sum(centered * centered, axis=1), "tensor") / D
    target = (centered * lax.rsqrt(var + 1e-06)[:, None]).astype(jnp.bfloat16)
    mask_count, tokens_pred, width_pred = pred_hidden.shape
    feature_cols = pred_weight.shape[1]
    devices = lax.axis_size("seq")
    clip_total = devices * tokens_here // CLIP
    flat_hidden = pred_hidden.reshape(mask_count * tokens_pred, width_pred)
    pred = jnp.dot(flat_hidden, pred_weight, preferred_element_type=jnp.float32).reshape(
        mask_count, tokens_pred, feature_cols
    )
    difference = pred - target.astype(jnp.float32)[None, :, :]
    error = (jnp.clip(difference, -1.0, 1.0) * mask.astype(jnp.float32)[:, :, None]).astype(
        jnp.bfloat16
    )
    error = error.reshape(mask_count * tokens_pred, feature_cols)
    grad_scale = 1.0 / math.sqrt(MASKS * clip_total * MASKED)
    columns = flat_hidden
    product = lax.dot_general(
        columns, error, (((0,), (0,)), ((), ())), preferred_element_type=jnp.float32
    )
    pred_grad = lax.psum_scatter(product * grad_scale, "seq", scatter_dimension=0, tiled=True)
    return (target, pred_grad)


def solution(mesh):
    placed = (
        P("seq", "tensor"),
        P("seq", "tensor"),
        P("seq", "tensor"),
        P("seq", "tensor"),
        P("seq", "tensor"),
        P(None, "seq", None),
        P(None, "tensor"),
        P(None, "seq"),
    )
    return jax.shard_map(
        body,
        mesh=mesh,
        in_specs=placed,
        out_specs=(P("seq", "tensor"), P("seq", "tensor")),
        check_vma=False,
    )
```

profile of v0, /device:TPU:128, one launch (start us, length us, event | category | flops | bytes accessed | tf_op | source)
XLA Modules:
  0.0 731.8 jit_solution(6433186562066900300)
XLA Ops:
  7.2 0.0 copy-start
  7.2 0.0 all-gather.2.cloned.1.call-start
  7.2 1.1 copy.60
  8.3 1.0 copy.57
  9.4 0.8 pad_maximum_fusion.3
  10.1 4.3 collective-permute-start
  14.4 4.9 collective-permute-done
  19.3 3.4 collective-permute-start.1
  22.7 8.8 %collective-permute-done.1 = bf16[2,256,384]{1,2,0:T(8,128)(2,1)S(1)} collective-permute-done((bf16[2,256,384]{1,2,0:T(8,128)(2,1)S(1)}, bf16[2,256,384]{1,2,0:T(8,128)(2,1)S(1)}, u32[]{:S(2)}, u32[]{:S(2)}) %collective-permute-start.1) | collective-permute-done | bytes 393248 | tf_op jit(solution)/shard_map/ppermute | solution.py:18
  31.5 1.0 pad_maximum_fusion.1
  32.5 4.9 collective-permute-start.2
  37.5 0.0 all-gather.2.cloned.1.call-update
  37.5 0.0 reduce-scatter.4.cloned.1.call-start
  37.5 16.4 %collective-permute-done.2 = bf16[2,512,384]{1,2,0:T(8,128)(2,1)S(1)} collective-permute-done((bf16[2,512,384]{1,2,0:T(8,128)(2,1)}, bf16[2,512,384]{1,2,0:T(8,128)(2,1)S(1)}, u32[]{:S(2)}, u32[]{:S(2)}) %collective-permute-start.2) | collective-permute-done | bytes 786464 | tf_op jit(solution)/shard_map/ppermute | solution.py:18
  53.9 0.2 pad_maximum_fusion
  54.2 0.0 copy-start.5
  54.2 0.0 copy-start.6
  54.2 3.6 collective-permute-start.3
  57.8 0.7 constant_dynamic-update-slice_fusion.3
  58.5 0.8 constant_dynamic-update-slice_fusion.2
  59.4 1.0 constant_dynamic-update-slice_fusion.1
  60.4 37.6 %collective-permute-done.3 = bf16[2,1024,384]{1,2,0:T(8,128)(2,1)S(1)} collective-permute-done((bf16[2,1024,384]{1,2,0:T(8,128)(2,1)S(1)}, bf16[2,1024,384]{1,2,0:T(8,128)(2,1)S(1)}, u32[]{:S(2)}, u32[]{:S(2)}) %collective-permute-start.3) | collective-permute-done | bytes 1572896 | tf_op jit(solution)/shard_map/ppermute | solution.py:18
  98.0 1.1 copy-done.1
  99.1 1.3 constant_dynamic-update-slice_fusion
  100.4 4.6 collective-permute-start.4
  105.0 0.0 copy-done.5
  105.0 0.1 copy.56
  105.1 0.0 copy-done.6
  105.1 0.0 copy-start.2
  105.2 0.3 fusion.91
  105.4 0.3 fusion.90
  105.8 0.3 fusion.89
  106.1 0.1 fusion.85
  106.1 0.3 fusion.88
  106.5 0.1 copy-done.2
  106.5 0.1 fusion.84
  106.7 0.5 bitcast_reduce_fusion.1
  107.1 150.8 %collective-permute-done.4 = bf16[2,2048,384]{1,2,0:T(8,128)(2,1)} collective-permute-done((bf16[2,2048,384]{1,2,0:T(8,128)(2,1)}, bf16[2,2048,384]{1,2,0:T(8,128)(2,1)}, u32[]{:S(2)}, u32[]{:S(2)}) %collective-permute-start.4) | collective-permute-done | bytes 3145760 | tf_op jit(solution)/shard_map/ppermute | solution.py:18
  258.0 2.3 fusion.83
  260.2 0.7 bitcast_reduce_fusion
  261.0 0.1 fusion.59
  261.0 0.2 fusion.61
  261.2 0.1 fusion.55
  261.3 0.1 fusion.47
  261.5 0.2 fusion.10
  261.7 0.4 fusion.2
  262.1 0.2 fusion.34
  262.3 0.3 fusion.36
  262.6 0.2 fusion.30
  262.9 0.4 convolution_bitcast_fusion.4
  263.3 0.0 copy-start.4
  263.3 0.7 fusion.41
  264.0 0.3 fusion.44
  264.3 19.6 %all_gather.6 = bf16[128,3072]{0,1:T(8,128)(2,1)S(1)} all-gather(bf16[128,384]{0,1:T(8,128)(2,1)S(1)} %bitcast.236), channel_id=1, replica_groups=mesh['seq'=64,'tensor'=8] {'tensor'}, dimensions={1}, use_global_device_ids=true | all-gather | bytes 884736 | tf_op jit(solution)/shard_map/all_gather | solution.py:70
  284.0 84.9 %all-gather.2.cloned.1.call-done = bf16[3072,768]{1,0:T(8,128)(2,1)} async-done(((bf16[48,768]{1,0:T(8,128)(2,1)}), bf16[3072,768]{1,0:T(8,128)(2,1)}) %all-gather.2.cloned.1.call-update) | async-done | bytes 4718608 | tf_op jit(solution)/shard_map/all_gather | solution.py:74
  368.9 3.2 fusion.92
  372.1 12.1 %psum.14 = f32[128]{0:T(128)S(1)} all-reduce(f32[128]{0:T(128)S(1)} %get-tuple-element.47), channel_id=1, replica_groups=mesh['seq'=64,'tensor'=8] {'tensor'}, use_global_device_ids=true, to_apply=%region_13.0 | all-reduce | flops 128 | bytes 1024 | tf_op jit(solution)/shard_map/psum | solution.py:78
  384.2 0.2 multiply_reduce_fusion
  384.4 13.3 %psum.15 = f32[128]{0:T(128)S(1)} all-reduce(f32[128]{0:T(128)S(1)} %multiply_reduce_fusion), channel_id=1, replica_groups=mesh['seq'=64,'tensor'=8] {'tensor'}, use_global_device_ids=true, to_apply=%region_15.0 | all-reduce | flops 128 | bytes 1024 | tf_op jit(solution)/shard_map/psum | solution.py:80
  397.7 0.8 fusion.79
  398.5 3.1 fusion
  401.6 3.6 copy.100
  405.2 0.0 reduce-scatter.4.cloned.1.call-update
  405.2 319.8 %reduce-scatter.4.cloned.1.call-done = f32[16,768]{1,0:T(8,128)} async-done(((f32[1024,768]{1,0:T(8,128)}), f32[16,768]{1,0:T(8,128)}) %reduce-scatter.4.cloned.1.call-update) | async-done | bytes 49168
  (13 shorter events, 0.2 us)
Async XLA Ops:
  7.2 391.4 %copy-start = (bf16[1024,768]{1,0:T(8,128)(2,1)S(1)}, bf16[1024,768]{1,0:T(8,128)(2,1)}, u32[]{:S(2)}) copy-start(bf16[1024,768]{1,0:T(8,128)(2,1)} %param.14) | copy-start | bytes 4718596
  7.2 361.7 %all-gather.2.cloned.1.call-start = ((), (), s32[]{:S(2)}) async-start(), calls=%async_computation.1 | async-start | bytes 4792320 | tf_op jit(solution)/shard_map/all_gather | solution.py:74
  10.1 9.2 %collective-permute-start = (bf16[2,128,384]{1,2,0:T(8,128)(2,1)S(1)}, bf16[2,128,384]{1,2,0:T(8,128)(2,1)S(1)}, u32[]{:S(2)}, u32[]{:S(2)}) collective-permute-start(bf16[2,128,384]{1,2,0:T(8,128)(2,1)S(1)} %get-tuple-element.30), channel_id=1, source_target_pairs={{0,8},{8,0},{16,24},{24,16},{32,40},{40,32},{48,56},{56,48},{64,72... | collective-permute-start | bytes 589832 | tf_op jit(solution)/shard_map/ppermute | solution.py:18
  19.3 12.2 %collective-permute-start.1 = (bf16[2,256,384]{1,2,0:T(8,128)(2,1)S(1)}, bf16[2,256,384]{1,2,0:T(8,128)(2,1)S(1)}, u32[]{:S(2)}, u32[]{:S(2)}) collective-permute-start(bf16[2,256,384]{1,2,0:T(8,128)(2,1)S(1)} %pad_maximum_fusion.2), channel_id=1, source_target_pairs={{0,16},{8,24},{16,0},{24,8},{32,48},{40,56},{48,32},{56,40},{64,80... | collective-permute-start | bytes 1179656 | tf_op jit(solution)/shard_map/ppermute | solution.py:18
  32.5 21.4 %collective-permute-start.2 = (bf16[2,512,384]{1,2,0:T(8,128)(2,1)}, bf16[2,512,384]{1,2,0:T(8,128)(2,1)S(1)}, u32[]{:S(2)}, u32[]{:S(2)}) collective-permute-start(bf16[2,512,384]{1,2,0:T(8,128)(2,1)} %pad_maximum_fusion.1), channel_id=1, source_target_pairs={{0,32},{8,40},{16,48},{24,56},{32,0},{40,8},{48,16},{56,24},{64,96... | collective-permute-start | bytes 2359304 | tf_op jit(solution)/shard_map/ppermute | solution.py:18
  37.5 687.5 %reduce-scatter.4.cloned.1.call-start = ((), (), s32[]{:S(2)}) async-start(), calls=%async_computation.2 | async-start | bytes 3194880
  54.2 50.8 %copy-start.5 = (bf16[128,384]{1,0:T(8,128)(2,1)S(1)}, bf16[128,384]{1,0:T(8,128)(2,1)}, u32[]{:S(2)}) copy-start(bf16[128,384]{1,0:T(8,128)(2,1)} %param.8) | copy-start | bytes 294916
  54.2 51.0 %copy-start.6 = (s32[2,128]{1,0:T(2,128)S(1)}, s32[2,128]{1,0:T(2,128)}, u32[]{:S(2)}) copy-start(s32[2,128]{1,0:T(2,128)} %param.15) | copy-start | bytes 3076
  54.2 43.8 %collective-permute-start.3 = (bf16[2,1024,384]{1,2,0:T(8,128)(2,1)S(1)}, bf16[2,1024,384]{1,2,0:T(8,128)(2,1)S(1)}, u32[]{:S(2)}, u32[]{:S(2)}) collective-permute-start(bf16[2,1024,384]{1,2,0:T(8,128)(2,1)S(1)} %pad_maximum_fusion), channel_id=1, source_target_pairs={{0,64},{8,72},{16,80},{24,88},{32,96},{40,104},{48,112},{56,120},{... | collective-permute-start | bytes 4718600 | tf_op jit(solution)/shard_map/ppermute | solution.py:18
  98.0 1.1 copy-start.1
  100.4 157.5 %collective-permute-start.4 = (bf16[2,2048,384]{1,2,0:T(8,128)(2,1)}, bf16[2,2048,384]{1,2,0:T(8,128)(2,1)}, u32[]{:S(2)}, u32[]{:S(2)}) collective-permute-start(bf16[2,2048,384]{1,2,0:T(8,128)(2,1)} %constant_dynamic-update-slice_fusion), channel_id=1, source_target_pairs={{0,128},{8,136},{16,144},{24,152},{32,160},{40,168},{48,176},{56,1... | collective-permute-start | bytes 9437192 | tf_op jit(solution)/shard_map/ppermute | solution.py:18
  105.1 1.4 copy-start.2
  263.3 105.6 %copy-start.4 = (bf16[128,768]{1,0:T(8,128)(2,1)S(1)}, bf16[128,768]{1,0:T(8,128)(2,1)}, u32[]{:S(2)}) copy-start(bf16[128,768]{1,0:T(8,128)(2,1)} %param.11) | copy-start | bytes 589828
  284.0 114.6 %copy-start.3 = (bf16[2,128,1024]{2,1,0:T(8,128)(2,1)S(1)}, bf16[2,128,1024]{2,1,0:T(8,128)(2,1)}, u32[]{:S(2)}) copy-start(bf16[2,128,1024]{2,1,0:T(8,128)(2,1)} %param.13) | copy-start | bytes 1572868
Sparse Core Ops, SparseCore 0:
  37.6 331.2 all-gather.1
  405.3 319.5 reduce-scatter.3
where the time goes:
time: 732 us
  waiting for transfers between devices  623 us (85%)
  blocking collectives  45 us (6%)
  starting transfers between devices  20.9 us (3%)
  between operations  14.3 us (2%)
  local copies, waits for them, and re-layouts  13.4 us (2%)
  matrix products  10.8 us (1%)
    unnamed x3, waiting for transfers between devices  320 us
    ppermute x5, waiting for transfers between devices, swapped(): return lax.ppermute(value, axis, pairs)  219 us
    all_gather x1, waiting for transfers between devices, body(): lax.all_gather(out_weight, 'seq', axis=0, tiled=True)  84.9 us
    ppermute x5, starting transfers between devices, swapped(): return lax.ppermute(value, axis, pairs)  20.8 us
    all_gather x1, blocking collectives, body(): attended_all = lax.all_gather(attended, 'tensor', axis=1, tiled=True)  19.6 us
  transfers between devices with their start and end apart: 7, of which 7 were waited for; matrix products, arithmetic and copies ran while one was open for 2% of the time, Pallas kernels for 0%

commit v1 on v0

v1 whole, which is shorter than its diff:
```python
import functools
import math

import jax
import jax.numpy as jnp
from jax import lax
from jax.experimental import pallas as pl
from jax.experimental.pallas import tpu as pltpu
from jax.sharding import Mesh
from jax.sharding import PartitionSpec as P

D = 6144
HD = 128
CLIP = 4096
MASKS = 2
MASKED = 3072
HEADS_HERE = 3
SEQ = ("h", "y", "x", "z")
TENSOR = ("w", "c")
LOG2E_ROOT = math.log2(math.e) / math.sqrt(HD)


def ring(size, distance):
    return [(source, (source + distance) % size) for source in range(size)]


def column_to_row(column):
    size = column.shape[0]
    rows = lax.broadcasted_iota(jnp.int32, (size, size), 0)
    cols = lax.broadcasted_iota(jnp.int32, (size, size), 1)
    return jnp.sum(jnp.where(rows == cols, column, 0.0), axis=0, keepdims=True)


def row_to_column(row):
    size = row.shape[1]
    rows = lax.broadcasted_iota(jnp.int32, (size, size), 0)
    cols = lax.broadcasted_iota(jnp.int32, (size, size), 1)
    return jnp.sum(jnp.where(rows == cols, row, 0.0), axis=1, keepdims=True)


def attend_kernel(q_own, q_far, kv0, kv1, kv2, kv3, own, far):
    parts = (kv0, kv1, kv2, kv3)
    keys = jnp.concatenate([p[i, 0] for p in parts for i in range(p.shape[0])], axis=0)
    values = jnp.concatenate([p[i, 1] for p in parts for i in range(p.shape[0])], axis=0)
    for q_ref, out in ((q_own, own), (q_far, far)):
        count = q_ref.shape[0]
        out[count * HD :, :] = jnp.zeros((8, HD), jnp.float32)
        for block in range(0, count, 2):
            query = jnp.concatenate([q_ref[block], q_ref[block + 1]], axis=0)
            scores = lax.dot_general(
                query, keys, (((1,), (1,)), ((), ())), preferred_element_type=jnp.float32
            )
            best = jnp.max(scores, axis=1, keepdims=True)
            exponent = jnp.exp2((scores - best) * LOG2E_ROOT)
            total = jnp.sum(exponent, axis=1, keepdims=True)
            summed = jnp.dot(
                exponent.astype(jnp.bfloat16), values, preferred_element_type=jnp.float32
            )
            out[block * HD : (block + 2) * HD, :] = summed / total
            level = best * LOG2E_ROOT + jnp.log2(total)
            out[count * HD + block : count * HD + block + 1, :] = column_to_row(level[:HD])
            out[count * HD + block + 1 : count * HD + block + 2, :] = column_to_row(level[HD:])


def combine_kernel(one, two, out):
    count = out.shape[0] // HD
    for block in range(count):
        level_one = row_to_column(one[count * HD + block : count * HD + block + 1, :])
        level_two = row_to_column(two[count * HD + block : count * HD + block + 1, :])
        best = jnp.maximum(level_one, level_two)
        weight_one = jnp.exp2(level_one - best)
        weight_two = jnp.exp2(level_two - best)
        rows = slice(block * HD, (block + 1) * HD)
        out[rows, :] = (
            (weight_one * one[rows, :] + weight_two * two[rows, :]) / (weight_one + weight_two)
        ).astype(jnp.bfloat16)


VMEM = pl.BlockSpec(memory_space=pltpu.VMEM)


def attend(q_own, q_far, kvs):
    rows = q_own.shape[0] * HD + 8
    shape = jax.ShapeDtypeStruct((rows, HD), jnp.float32)
    return pl.pallas_call(
        attend_kernel,
        out_shape=(shape, shape),
        in_specs=[VMEM] * 6,
        out_specs=(VMEM, VMEM),
        compiler_params=pltpu.CompilerParams(vmem_limit_bytes=40 * 1024 * 1024),
        cost_estimate=pl.CostEstimate(
            flops=4 * 1024 * 2048 * HD, bytes_accessed=2**21, transcendentals=1024 * 2048
        ),
    )(q_own, q_far, *kvs)


def combine(one, two):
    return pl.pallas_call(
        combine_kernel,
        out_shape=jax.ShapeDtypeStruct((one.shape[0] - 8, HD), jnp.bfloat16),
        in_specs=[VMEM] * 2,
        out_specs=VMEM,
    )(one, two)


def by_head(array):
    tokens = array.shape[0]
    heads = array.reshape(tokens, HEADS_HERE, HD).transpose(1, 0, 2)
    return jnp.concatenate([heads, heads[2:]], axis=0)


def body(queries, keys, values, residual, out_weight, pred_hidden, pred_weight, mask):
    tokens_here = queries.shape[0]
    packed = jnp.stack((by_head(keys), by_head(values), by_head(queries)), axis=1)
    packed = lax.all_to_all(packed, "y", 0, 0, tiled=True)
    kv_own = packed[:, :2]
    q_own = packed[:, 2]
    kvs = [kv_own] + [lax.ppermute(kv_own, "x", ring(4, d)) for d in (2, 1, 3)]
    q_far = lax.ppermute(q_own, "z", ring(2, 1))

    weight_rows = lax.all_gather(out_weight, "z", axis=0, tiled=True)
    weight_rows = lax.all_gather(weight_rows, "x", axis=0, tiled=True)
    weight_heads = weight_rows.reshape(HEADS_HERE, HD, -1)
    weight_heads = jnp.concatenate([weight_heads, weight_heads[2:]], axis=0)
    weight_heads = jnp.concatenate([weight_heads, weight_heads], axis=0)
    weight_here = lax.all_to_all(weight_heads, ("h", "y"), 0, 0, tiled=True)

    own, far = attend(q_own, q_far, kvs)
    arrived = lax.ppermute(far, "z", ring(2, 1))
    attended = combine(own, arrived)

    every = lax.all_gather(attended, "w", axis=0)
    every = lax.all_gather(every, "c", axis=1)
    columns = every.reshape(8, 4 * tokens_here, HD).transpose(1, 0, 2).reshape(4 * tokens_here, 8 * HD)
    part = jnp.dot(
        columns, weight_here.reshape(8 * HD, -1), preferred_element_type=jnp.float32
    )
    part = part.astype(jnp.bfloat16).reshape(4, tokens_here, -1)
    part = lax.all_to_all(part, "y", 0, 0, tiled=True)
    projected = (
        part[0].astype(jnp.float32) + part[1].astype(jnp.float32) + part[2].astype(jnp.float32)
    )
    summed = residual.astype(jnp.float32) + projected

    width = summed.shape[1]
    mean_here = jnp.sum(summed, axis=1) / width
    off = summed - mean_here[:, None]
    square_here = jnp.sum(off * off, axis=1)
    both = lax.all_gather(jnp.stack((mean_here, square_here)), TENSOR, axis=0)
    mean = jnp.sum(both[:, 0], axis=0) * (width / D)
    shift = both[:, 0] - mean[None, :]
    var = jnp.sum(both[:, 1] + width * shift * shift, axis=0) / D
    target = ((summed - mean[:, None]) * lax.rsqrt(var + 1e-06)[:, None]).astype(jnp.bfloat16)

    mask_count, tokens_pred, width_pred = pred_hidden.shape
    clip_total = 2
    flat_hidden = pred_hidden.reshape(mask_count * tokens_pred, width_pred)
    pred = jnp.dot(flat_hidden, pred_weight, preferred_element_type=jnp.float32).reshape(
        mask_count, tokens_pred, width
    )
    difference = pred - target.astype(jnp.float32)[None, :, :]
    error = (jnp.clip(difference, -1.0, 1.0) * mask.astype(jnp.float32)[:, :, None]).astype(
        jnp.bfloat16
    )
    error = error.reshape(mask_count * tokens_pred, width)
    grad_scale = 1.0 / math.sqrt(MASKS * clip_total * MASKED)
    product = lax.dot_general(
        flat_hidden, error, (((0,), (0,)), ((), ())), preferred_element_type=jnp.float32
    )
    product = product.astype(jnp.bfloat16).reshape(64, -1, width)
    product = lax.all_to_all(product, SEQ, 0, 0, tiled=True)
    pred_grad = jnp.sum(product.astype(jnp.float32), axis=0) * grad_scale
    return (target, pred_grad)


def solution(mesh):
    fine = Mesh(mesh.devices.reshape(2, 4, 4, 2, 4, 2), SEQ + TENSOR)
    placed = (
        P(SEQ, TENSOR),
        P(SEQ, TENSOR),
        P(SEQ, TENSOR),
        P(SEQ, TENSOR),
        P(SEQ, TENSOR),
        P(None, SEQ, None),
        P(None, TENSOR),
        P(None, SEQ),
    )
    return jax.shard_map(
        body,
        mesh=fine,
        in_specs=placed,
        out_specs=(P(SEQ, TENSOR), P(SEQ, TENSOR)),
        check_vma=False,
    )
```

time: 732 us -> 219 us (0.30)
  the two profiles are of different devices: /device:TPU:128 before, /device:TPU:8 now
where the time goes in v1:
time: 219 us; the launch traced here: 218 us
  blocking collectives  104 us (47%)
  waiting for transfers between devices  42 us (19%)
  starting transfers between devices  34.5 us (16%)
  between operations  14.2 us (6%)
  matrix products  6.9 us (3%)
  local copies, waits for them, and re-layouts  6.73 us (3%)
  Pallas kernels  5.28 us (2%)
  other arithmetic  4.36 us (2%)
    all_to_all x1, blocking collectives, body(): product = lax.all_to_all(product, SEQ, 0, 0, tiled=True)  52.3 us
    all_gather x1, blocking collectives, body(): every = lax.all_gather(attended, 'w', axis=0)  20.6 us
    all_to_all x1, waiting for transfers between devices, body(): part = lax.all_to_all(part, 'y', 0, 0, tiled=True)  17.4 us
    all_gather x1, waiting for transfers between devices, body(): every = lax.all_gather(every, 'c', axis=1)  13.9 us
    all_gather x1, blocking collectives, body(): both = lax.all_gather(jnp.stack((mean_here, square_here)), TENSOR, axis=0)  13.2 us
    all_gather x1, blocking collectives, body(): weight_rows = lax.all_gather(weight_rows, 'x', axis=0, tiled=True)  13.1 us
    ppermute x3, starting transfers between devices, body(): kvs = [kv_own] + [lax.ppermute(kv_own, 'x', ring(4, d)) for d in (2, 1, 3)]  10.4 us
    all_to_all x1, starting transfers between devices, body(): packed = lax.all_to_all(packed, 'y', 0, 0, tiled=True)  9.25 us
  transfers between devices with their start and end apart: 9, of which 4 were waited for; matrix products, arithmetic and copies ran while one was open for 1% of the time, Pallas kernels for 2%

profile of v1, /device:TPU:8, one launch (start us, length us, event | category | flops | bytes accessed | tf_op | source)
XLA Modules:
  0.0 218.4 jit_solution(18055949336027663958)
XLA Ops:
  7.2 0.0 copy-start
  7.2 1.1 copy.21
  8.3 0.1 copy.22
  8.5 1.0 copy.23
  9.5 0.0 copy-start.4
  9.5 0.1 copy.24
  9.6 1.0 copy.25
  10.6 0.1 copy.26
  10.8 0.8 pad_maximum_fusion.1
  11.6 9.2 %all-to-all-start = ((bf16[4,3,128,128]{3,2,1,0:T(8,128)(2,1)}), bf16[4,3,128,128]{3,2,1,0:T(8,128)(2,1)S(1)}, u32[]{:S(2)}, u32[]{:S(2)}) async-start(bf16[4,3,128,128]{3,2,1,0:T(8,128)(2,1)} %pad_maximum_fusion.1), calls=%async_computation | async-start | bytes 786432 | tf_op jit(solution)/shard_map/all_to_all | solution.py:115
  20.9 0.0 copy-done.4
  20.9 5.0 %all_gather.28 = bf16[96,768]{1,0:T(8,128)(2,1)S(1)} all-gather(bf16[48,768]{1,0:T(8,128)(2,1)S(1)} %copy-done.4), channel_id=1, replica_groups=mesh['h'=2,'y'=4,'x'=4,'z'=2,'w'=4,'c'=2] {'z'}, dimensions={0}, use_global_device_ids=true | all-gather | bytes 221184 | tf_op jit(solution)/shard_map/all_gather | solution.py:121
  25.9 13.1 %all_gather.29 = bf16[384,768]{1,0:T(8,128)(2,1)S(1)} all-gather(bf16[96,768]{1,0:T(8,128)(2,1)S(1)} %all_gather.28), channel_id=1, replica_groups=mesh['h'=2,'y'=4,'x'=4,'z'=2,'w'=4,'c'=2] {'x'}, dimensions={0}, use_global_device_ids=true | all-gather | bytes 737280 | tf_op jit(solution)/shard_map/all_gather | solution.py:122
  39.1 1.4 pad_maximum_fusion
  40.4 0.0 all-to-all-done
  40.4 5.1 %all-to-all-start.1 = ((bf16[8,128,768]{2,1,0:T(8,128)(2,1)}), bf16[8,128,768]{2,1,0:T(8,128)(2,1)S(1)}, u32[]{:S(2)}, u32[]{:S(2)}) async-start(bf16[8,128,768]{2,1,0:T(8,128)(2,1)} %pad_maximum_fusion), calls=%async_computation.1 | async-start | bytes 3145728 | tf_op jit(solution)/shard_map/all_to_all | solution.py:126
  45.5 0.0 all-gather.6.cloned.1.call-start
  45.5 3.4 %collective-permute-start.1 = (bf16[4,2,128,128]{3,2,1,0:T(8,128)(2,1)S(1)}, bf16[4,2,128,128]{3,2,1,0:T(8,128)(2,1)S(1)}, u32[]{:S(2)}, u32[]{:S(2)}) collective-permute-start(bf16[4,2,128,128]{3,2,1,0:T(8,128)(2,1)S(1)} %slice.53.kv0), channel_id=1, source_target_pairs={{0,32},{16,48},{32,0},{48,16},{1,33},{17,49},{33,1},{49,17},{2,34}... | collective-permute-start | bytes 786440 | tf_op jit(solution)/shard_map/ppermute | solution.py:118
  48.9 2.0 collective-permute-start.2
  50.9 5.1 %collective-permute-start.3 = (bf16[4,2,128,128]{3,2,1,0:T(8,128)(2,1)S(1)}, bf16[4,2,128,128]{3,2,1,0:T(8,128)(2,1)S(1)}, u32[]{:S(2)}, u32[]{:S(2)}) collective-permute-start(bf16[4,2,128,128]{3,2,1,0:T(8,128)(2,1)S(1)} %slice.53.kv0), channel_id=1, source_target_pairs={{0,48},{16,0},{32,16},{48,32},{1,49},{17,1},{33,17},{49,33},{2,50}... | collective-permute-start | bytes 786440 | tf_op jit(solution)/shard_map/ppermute | solution.py:118
  56.0 2.2 %collective-permute-start = (bf16[4,128,128]{2,1,0:T(8,128)(2,1)S(1)}, bf16[4,128,128]{2,1,0:T(8,128)(2,1)S(1)}, u32[]{:S(2)}, u32[]{:S(2)}) collective-permute-start(bf16[4,128,128]{2,1,0:T(8,128)(2,1)S(1)} %slice_bitcast_fusion.1.q_own), channel_id=1, source_target_pairs={{0,8},{8,0},{1,9},{9,1},{2,10},{10,2},{3,11},{11,3},{4,12},{12,4},... | collective-permute-start | bytes 393224 | tf_op jit(solution)/shard_map/ppermute | solution.py:119
  58.3 4.6 %collective-permute-done.q_far = bf16[4,128,128]{2,1,0:T(8,128)(2,1)S(1)} collective-permute-done((bf16[4,128,128]{2,1,0:T(8,128)(2,1)S(1)}, bf16[4,128,128]{2,1,0:T(8,128)(2,1)S(1)}, u32[]{:S(2)}, u32[]{:S(2)}) %collective-permute-start) | collective-permute-done | bytes 131104 | tf_op jit(solution)/shard_map/ppermute | solution.py:119
  62.9 0.0 collective-permute-done.1.kv1
  62.9 0.0 collective-permute-done.2.kv2
  62.9 0.0 collective-permute-done.3.kv3
  62.9 3.4 %shard_map.95 = (f32[520,128]{1,0:T(8,128)S(1)}, f32[520,128]{1,0:T(8,128)S(1)}) custom-call(bf16[4,128,128]{2,1,0:T(8,128)(2,1)S(1)} %slice_bitcast_fusion.1.q_own, bf16[4,128,128]{2,1,0:T(8,128)(2,1)S(1)} %collective-permute-done.q_far, bf16[4,2,128,128]{3,2,1,0:T(8,128)(2,1)S(1)} %slice.53.kv0, bf16[4,2,128,128]{3,2,1,0:T(8,128)(2,1)S(1)} %collective-permute-done.1.kv1, ...), custom_call_target="tpu_custom_call" | custom-call | flops 1073741824 | bytes 2097152 | tf_op jit(solution)/shard_map/pallas_call | solution.py:85
  66.2 0.0 copy-start.1
  66.3 0.7 copy-done.1
  66.9 2.2 %collective-permute-start.4 = (f32[520,128]{1,0:T(8,128)S(1)}, f32[520,128]{1,0:T(8,128)S(1)}, u32[]{:S(2)}, u32[]{:S(2)}) collective-permute-start(f32[520,128]{1,0:T(8,128)S(1)} %get-tuple-element.5), channel_id=1, source_target_pairs={{0,8},{8,0},{1,9},{9,1},{2,10},{10,2},{3,11},{11,3},{4,12},{12,4},... | collective-permute-start | bytes 798728 | tf_op jit(solution)/shard_map/ppermute | solution.py:129
  69.2 6.1 %collective-permute-done.4.two = f32[520,128]{1,0:T(8,128)S(1)} collective-permute-done((f32[520,128]{1,0:T(8,128)S(1)}, f32[520,128]{1,0:T(8,128)S(1)}, u32[]{:S(2)}, u32[]{:S(2)}) %collective-permute-start.4) | collective-permute-done | bytes 266272 | tf_op jit(solution)/shard_map/ppermute | solution.py:129
  75.2 0.0 copy-start.3
  75.2 0.7 copy-done.3
  76.0 1.9 shard_map.96
  77.9 20.6 %all-gather = bf16[2048,128]{1,0:T(8,128)(2,1)} all-gather(bf16[512,128]{1,0:T(8,128)(2,1)} %shard_map.96), channel_id=2, replica_groups=mesh['h'=2,'y'=4,'x'=4,'z'=2,'w'=4,'c'=2] {'w'}, dimensions={0}, use_global_device_ids=true | all-gather | bytes 655360 | tf_op jit(solution)/shard_map/all_gather | solution.py:132
  98.5 0.0 all-gather.6.cloned.1.call-update
  98.6 13.9 %all-gather.6.cloned.1.call-done = bf16[4,1024,128]{2,1,0:T(8,128)(2,1)} async-done(((bf16[4,512,128]{2,1,0:T(8,128)(2,1)}), bf16[4,1024,128]{2,1,0:T(8,128)(2,1)}) %all-gather.6.cloned.1.call-update) | async-done | bytes 1048592 | tf_op jit(solution)/shard_map/all_gather | solution.py:133
  112.4 0.0 all-to-all-done.1
  112.4 3.1 %bitcast_convert_fusion.1 = bf16[512,768]{1,0:T(8,128)(2,1)} fusion(bf16[512,8,128]{2,0,1:T(8,128)(2,1)} %bitcast.82, bf16[8,128,768]{2,1,0:T(8,128)(2,1)S(1)} %all-to-all-done.1), kind=kOutput, calls=%fused_computation.5 | convolution fusion | flops 805699584 | bytes 3407872 | tf_op jit(solution)/shard_map/dot_general | solution.py:135
  115.5 0.0 copy-start.5
  115.5 0.0 copy-start.2
  115.5 5.3 %all-to-all-start.2 = ((bf16[4,128,768]{2,1,0:T(8,128)(2,1)}), bf16[4,128,768]{2,1,0:T(8,128)(2,1)S(1)}, u32[]{:S(2)}, u32[]{:S(2)}) async-start(bf16[4,128,768]{2,1,0:T(8,128)(2,1)} %bitcast.69), calls=%async_computation.2 | async-start | bytes 1572864 | tf_op jit(solution)/shard_map/all_to_all | solution.py:139
  120.8 0.0 copy-done.5
  120.8 17.4 %all-to-all-done.2 = bf16[4,128,768]{2,1,0:T(8,128)(2,1)S(1)} async-done(((bf16[4,128,768]{2,1,0:T(8,128)(2,1)}), bf16[4,128,768]{2,1,0:T(8,128)(2,1)S(1)}, u32[]{:S(2)}, u32[]{:S(2)}) %all-to-all-start.2) | async-done | bytes 786464 | tf_op jit(solution)/shard_map/all_to_all | solution.py:139
  138.2 0.0 copy-done.2
  138.2 0.2 fusion.26
  138.4 0.2 multiply_reduce_fusion
  138.7 13.2 %all-gather.3 = f32[8,2,128]{2,1,0:T(2,128)S(1)} all-gather(f32[1,2,128]{2,1,0:T(2,128)S(1)} %maximum_bitcast_fusion.3), channel_id=4, replica_groups=mesh['h'=2,'y'=4,'x'=4,'z'=2,'w'=4,'c'=2] {'w','c'}, dimensions={0}, use_global_device_ids=true | all-gather | bytes 9216 | tf_op jit(solution)/shard_map/all_gather | solution.py:149
  151.9 0.8 fusion.27
  152.8 0.0 copy-done
  152.8 3.8 %fusion.2 = bf16[1024,768]{0,1:T(8,128)(2,1)} fusion(bf16[2,128,1024]{2,1,0:T(8,128)(2,1)} %param.13, bf16[1024,768]{1,0:T(8,128)(2,1)S(1)} %copy-done, f32[2,128]{1,0:T(2,128)S(1)} %convert_element_type.46, f32[128,768]{1,0:T(8,128)S(1)} %get-tuple-element.6), kind=kOutput, calls=%fused_computation.6 | convolution fusion | flops 806879232 | bytes 4064256 | tf_op jit(solution)/shard_map/dot_general | solution.py:167
  156.6 1.7 copy.29
  158.3 52.3 %all_to_all.20 = bf16[64,16,768]{2,1,0:T(8,128)(2,1)S(1)} all-to-all(bf16[64,16,768]{2,1,0:T(8,128)(2,1)S(1)} %bitcast.66), channel_id=1, replica_groups=mesh['h'=2,'y'=4,'x'=4,'z'=2,'w'=4,'c'=2] {'h','y','x','z'}, dimensions={0} | all-to-all | bytes 3145728 | tf_op jit(solution)/shard_map/all_to_all | solution.py:171
  210.7 0.2 convert_reduce_fusion
  210.9 0.6 broadcast_multiply_fusion
  (15 shorter events, 0.2 us)
Async XLA Ops:
  7.2 145.6 %copy-start = (bf16[1024,768]{1,0:T(8,128)(2,1)S(1)}, bf16[1024,768]{1,0:T(8,128)(2,1)}, u32[]{:S(2)}) copy-start(bf16[1024,768]{1,0:T(8,128)(2,1)} %param.14) | copy-start | bytes 4718596
  9.5 11.4 %copy-start.4 = (bf16[48,768]{1,0:T(8,128)(2,1)S(1)}, bf16[48,768]{1,0:T(8,128)(2,1)}, u32[]{:S(2)}) copy-start(bf16[48,768]{1,0:T(8,128)(2,1)} %param.12) | copy-start | bytes 221188
  11.6 28.8 %all-to-all-start = ((bf16[4,3,128,128]{3,2,1,0:T(8,128)(2,1)}), bf16[4,3,128,128]{3,2,1,0:T(8,128)(2,1)S(1)}, u32[]{:S(2)}, u32[]{:S(2)}) async-start(bf16[4,3,128,128]{3,2,1,0:T(8,128)(2,1)} %pad_maximum_fusion.1), calls=%async_computation | async-start | bytes 786432 | tf_op jit(solution)/shard_map/all_to_all | solution.py:115
  40.4 72.0 %all-to-all-start.1 = ((bf16[8,128,768]{2,1,0:T(8,128)(2,1)}), bf16[8,128,768]{2,1,0:T(8,128)(2,1)S(1)}, u32[]{:S(2)}, u32[]{:S(2)}) async-start(bf16[8,128,768]{2,1,0:T(8,128)(2,1)} %pad_maximum_fusion), calls=%async_computation.1 | async-start | bytes 3145728 | tf_op jit(solution)/shard_map/all_to_all | solution.py:126
  45.5 66.9 %all-gather.6.cloned.1.call-start = ((), (), s32[]{:S(2)}) async-start(), calls=%async_computation.4 | async-start | bytes 1572864 | tf_op jit(solution)/shard_map/all_gather | solution.py:133
  45.5 17.3 %collective-permute-start.1 = (bf16[4,2,128,128]{3,2,1,0:T(8,128)(2,1)S(1)}, bf16[4,2,128,128]{3,2,1,0:T(8,128)(2,1)S(1)}, u32[]{:S(2)}, u32[]{:S(2)}) collective-permute-start(bf16[4,2,128,128]{3,2,1,0:T(8,128)(2,1)S(1)} %slice.53.kv0), channel_id=1, source_target_pairs={{0,32},{16,48},{32,0},{48,16},{1,33},{17,49},{33,1},{49,17},{2,34}... | collective-permute-start | bytes 786440 | tf_op jit(solution)/shard_map/ppermute | solution.py:118
  48.9 14.0 %collective-permute-start.2 = (bf16[4,2,128,128]{3,2,1,0:T(8,128)(2,1)S(1)}, bf16[4,2,128,128]{3,2,1,0:T(8,128)(2,1)S(1)}, u32[]{:S(2)}, u32[]{:S(2)}) collective-permute-start(bf16[4,2,128,128]{3,2,1,0:T(8,128)(2,1)S(1)} %slice.53.kv0), channel_id=1, source_target_pairs={{0,16},{16,32},{32,48},{48,0},{1,17},{17,33},{33,49},{49,1},{2,18}... | collective-permute-start | bytes 786440 | tf_op jit(solution)/shard_map/ppermute | solution.py:118
  50.9 12.0 %collective-permute-start.3 = (bf16[4,2,128,128]{3,2,1,0:T(8,128)(2,1)S(1)}, bf16[4,2,128,128]{3,2,1,0:T(8,128)(2,1)S(1)}, u32[]{:S(2)}, u32[]{:S(2)}) collective-permute-start(bf16[4,2,128,128]{3,2,1,0:T(8,128)(2,1)S(1)} %slice.53.kv0), channel_id=1, source_target_pairs={{0,48},{16,0},{32,16},{48,32},{1,49},{17,1},{33,17},{49,33},{2,50}... | collective-permute-start | bytes 786440 | tf_op jit(solution)/shard_map/ppermute | solution.py:118
  56.0 6.9 %collective-permute-start = (bf16[4,128,128]{2,1,0:T(8,128)(2,1)S(1)}, bf16[4,128,128]{2,1,0:T(8,128)(2,1)S(1)}, u32[]{:S(2)}, u32[]{:S(2)}) collective-permute-start(bf16[4,128,128]{2,1,0:T(8,128)(2,1)S(1)} %slice_bitcast_fusion.1.q_own), channel_id=1, source_target_pairs={{0,8},{8,0},{1,9},{9,1},{2,10},{10,2},{3,11},{11,3},{4,12},{12,4},... | collective-permute-start | bytes 393224 | tf_op jit(solution)/shard_map/ppermute | solution.py:119
  66.2 0.7 copy-start.1
  66.9 8.3 %collective-permute-start.4 = (f32[520,128]{1,0:T(8,128)S(1)}, f32[520,128]{1,0:T(8,128)S(1)}, u32[]{:S(2)}, u32[]{:S(2)}) collective-permute-start(f32[520,128]{1,0:T(8,128)S(1)} %get-tuple-element.5), channel_id=1, source_target_pairs={{0,8},{8,0},{1,9},{9,1},{2,10},{10,2},{3,11},{11,3},{4,12},{12,4},... | collective-permute-start | bytes 798728 | tf_op jit(solution)/shard_map/ppermute | solution.py:129
  75.2 0.7 copy-start.3
  115.5 5.3 %copy-start.5 = (s32[2,128]{1,0:T(2,128)S(1)}, s32[2,128]{1,0:T(2,128)}, u32[]{:S(2)}) copy-start(s32[2,128]{1,0:T(2,128)} %param.15) | copy-start | bytes 3076
  115.5 22.7 %copy-start.2 = (bf16[128,768]{1,0:T(8,128)(2,1)S(1)}, bf16[128,768]{1,0:T(8,128)(2,1)}, u32[]{:S(2)}) copy-start(bf16[128,768]{1,0:T(8,128)(2,1)} %param.11) | copy-start | bytes 589828
  115.5 22.7 %all-to-all-start.2 = ((bf16[4,128,768]{2,1,0:T(8,128)(2,1)}), bf16[4,128,768]{2,1,0:T(8,128)(2,1)S(1)}, u32[]{:S(2)}, u32[]{:S(2)}) async-start(bf16[4,128,768]{2,1,0:T(8,128)(2,1)} %bitcast.69), calls=%async_computation.2 | async-start | bytes 1572864 | tf_op jit(solution)/shard_map/all_to_all | solution.py:139
Sparse Core Ops, SparseCore 0:
  98.7 13.7 all-gather.5

commit v2 on v1

v2 whole, which is shorter than its diff:
```python
import math

import jax
import jax.numpy as jnp
from jax import lax
from jax.experimental import pallas as pl
from jax.experimental.pallas import tpu as pltpu
from jax.sharding import Mesh
from jax.sharding import PartitionSpec as P

D = 6144
HD = 128
CLIPS = 2
MASKS = 2
MASKED = 3072
HEADS_HERE = 3
SEQ = ("h", "y", "x", "z")
TENSOR = ("w", "c")
LOG2E_ROOT = math.log2(math.e) / math.sqrt(HD)
LEVEL_ROWS = 16
VMEM = pl.BlockSpec(memory_space=pltpu.VMEM)
SMEM = pl.BlockSpec(memory_space=pltpu.SMEM)
ROOMY = pltpu.CompilerParams(vmem_limit_bytes=40 * 1024 * 1024)


def ring(size, distance):
    return [(source, (source + distance) % size) for source in range(size)]


def diagonal(size):
    rows = lax.broadcasted_iota(jnp.int32, (size, size), 0)
    return rows == lax.broadcasted_iota(jnp.int32, (size, size), 1)


def column_to_row(column):
    return jnp.sum(jnp.where(diagonal(column.shape[0]), column, 0.0), axis=0, keepdims=True)


def row_to_column(row):
    return jnp.sum(jnp.where(diagonal(row.shape[1]), row, 0.0), axis=1, keepdims=True)


def pack_kernel(queries, keys, values, out):
    for place in range(4):
        head = min(place, HEADS_HERE - 1)
        columns = slice(head * HD, (head + 1) * HD)
        out[place, 0] = keys[:, columns]
        out[place, 1] = values[:, columns]
        out[place, 2] = queries[:, columns]


def pack(queries, keys, values):
    tokens = queries.shape[0]
    return pl.pallas_call(
        pack_kernel,
        out_shape=jax.ShapeDtypeStruct((4, 3, tokens, HD), jnp.bfloat16),
        in_specs=[VMEM] * 3,
        out_specs=VMEM,
    )(queries, keys, values)


def attend_kernel(here, q_own, q_far, kv0, kv1, kv2, kv3, out):
    parts = (kv0, kv1, kv2, kv3)
    keys = jnp.concatenate([p[i, 0] for p in parts for i in range(p.shape[0])], axis=0)
    values = jnp.concatenate([p[i, 1] for p in parts for i in range(p.shape[0])], axis=0)
    for q_ref, place in ((q_own, here[0]), (q_far, 1 - here[0])):
        for block in range(0, q_ref.shape[0], 2):
            query = jnp.concatenate([q_ref[block], q_ref[block + 1]], axis=0)
            scores = lax.dot_general(
                query, keys, (((1,), (1,)), ((), ())), preferred_element_type=jnp.float32
            )
            best = jnp.max(scores, axis=1, keepdims=True)
            exponent = jnp.exp2((scores - best) * LOG2E_ROOT)
            total = jnp.sum(exponent, axis=1, keepdims=True)
            summed = jnp.dot(
                exponent.astype(jnp.bfloat16), values, preferred_element_type=jnp.float32
            )
            summed = (summed / total).astype(jnp.bfloat16)
            level = best * LOG2E_ROOT + jnp.log2(total)
            for half in range(2):
                rows = slice(half * HD, (half + 1) * HD)
                row = column_to_row(level[rows])
                first = row.astype(jnp.bfloat16).astype(jnp.float32)
                second = (row - first).astype(jnp.bfloat16).astype(jnp.float32)
                third = row - first - second
                terms = jnp.concatenate(
                    [first, second, third, jnp.zeros((LEVEL_ROWS - 3, HD), jnp.float32)], axis=0
                )
                chunk = 2 * (block + half) + place
                out[chunk, :HD, :] = summed[rows]
                out[chunk, HD:, :] = terms.astype(jnp.bfloat16)


def attend(here, q_own, q_far, kvs):
    chunks = 2 * q_own.shape[0]
    return pl.pallas_call(
        attend_kernel,
        out_shape=jax.ShapeDtypeStruct((chunks, HD + LEVEL_ROWS, HD), jnp.bfloat16),
        in_specs=[SMEM] + [VMEM] * 6,
        out_specs=VMEM,
        compiler_params=ROOMY,
        cost_estimate=pl.CostEstimate(
            flops=4 * 1024 * 2048 * HD, bytes_accessed=2**21, transcendentals=1024 * 2048
        ),
    )(here, q_own, q_far, *kvs)


def combine_kernel(chunks, out):
    for head in range(HEADS_HERE):
        levels = []
        for part in range(2):
            terms = chunks[2 * head + part, HD:, :].astype(jnp.float32)
            levels.append(row_to_column(terms[0:1] + terms[1:2] + terms[2:3]))
        best = jnp.maximum(levels[0], levels[1])
        weights = [jnp.exp2(level - best) for level in levels]
        summed = sum(
            weights[part] * chunks[2 * head + part, :HD, :].astype(jnp.float32) for part in range(2)
        )
        out[:, head * HD : (head + 1) * HD] = (summed / (weights[0] + weights[1])).astype(
            jnp.bfloat16
        )


def combine(chunks):
    return pl.pallas_call(
        combine_kernel,
        out_shape=jax.ShapeDtypeStruct((HD, HEADS_HERE * HD), jnp.bfloat16),
        in_specs=[VMEM],
        out_specs=VMEM,
    )(chunks)


def project_kernel(columns, weight, residual, summed, stats, total):
    step = pl.program_id(0)
    product = jnp.dot(columns[0], weight[...], preferred_element_type=jnp.float32)

    @pl.when(step == 0)
    def _():
        total[...] = residual[...].astype(jnp.float32) + product

    @pl.when(step > 0)
    def _():
        total[...] += product

    @pl.when(step == pl.num_programs(0) - 1)
    def _():
        value = total[...]
        summed[...] = value
        mean = jnp.sum(value, axis=1, keepdims=True) / value.shape[1]
        off = value - mean
        stats[0:1, :] = column_to_row(mean)
        stats[1:2, :] = column_to_row(jnp.sum(off * off, axis=1, keepdims=True))


def project(columns, weight, residual):
    pieces, tokens, depth = columns.shape
    width = weight.shape[1]
    return pl.pallas_call(
        project_kernel,
        grid=(pieces,),
        out_shape=(
            jax.ShapeDtypeStruct((tokens, width), jnp.float32),
            jax.ShapeDtypeStruct((2, tokens), jnp.float32),
        ),
        in_specs=[
            pl.BlockSpec((1, tokens, depth), lambda i: (i, 0, 0)),
            pl.BlockSpec((depth, width), lambda i: (i, 0)),
            pl.BlockSpec((tokens, width), lambda i: (0, 0)),
        ],
        out_specs=(
            pl.BlockSpec((tokens, width), lambda i: (0, 0)),
            pl.BlockSpec((2, tokens), lambda i: (0, 0)),
        ),
        scratch_shapes=[pltpu.VMEM((tokens, width), jnp.float32)],
        compiler_params=ROOMY,
        cost_estimate=pl.CostEstimate(
            flops=2 * tokens * depth * pieces * width,
            bytes_accessed=2 * depth * pieces * width,
            transcendentals=0,
        ),
    )(columns, weight, residual)


def finish_kernel(stats, summed, pred, hidden, mask, target, product):
    width = summed.shape[1]
    tokens = summed.shape[0]
    means = stats[:, 0, :]
    mean = jnp.sum(means, axis=0, keepdims=True) * (width / D)
    shift = means - mean
    var = jnp.sum(stats[:, 1, :] + width * shift * shift, axis=0, keepdims=True) / D
    scale = row_to_column(lax.rsqrt(var + 1e-06))
    value = ((summed[...] - row_to_column(mean)) * scale).astype(jnp.bfloat16)
    target[...] = value
    value = value.astype(jnp.float32)
    errors = []
    for k in range(MASKS):
        rows = slice(k * tokens, (k + 1) * tokens)
        marked = row_to_column(mask[k : k + 1, :].astype(jnp.float32))
        errors.append((jnp.clip(pred[rows, :] - value, -1.0, 1.0) * marked).astype(jnp.bfloat16))
    error = jnp.concatenate(errors, axis=0)
    step = 256
    for start in range(0, hidden.shape[0], step):
        product[start : start + step, :] = jnp.dot(
            hidden[start : start + step, :], error, preferred_element_type=jnp.float32
        ).astype(jnp.bfloat16)


def finish(stats, summed, pred, hidden, mask):
    tokens, width = summed.shape
    return pl.pallas_call(
        finish_kernel,
        out_shape=(
            jax.ShapeDtypeStruct((tokens, width), jnp.bfloat16),
            jax.ShapeDtypeStruct((hidden.shape[0], width), jnp.bfloat16),
        ),
        in_specs=[VMEM] * 5,
        out_specs=(VMEM, VMEM),
        compiler_params=ROOMY,
        cost_estimate=pl.CostEstimate(
            flops=2 * hidden.shape[0] * hidden.shape[1] * width,
            bytes_accessed=2**22,
            transcendentals=0,
        ),
    )(stats, summed, pred, hidden, mask)


def body(queries, keys, values, residual, out_weight, pred_hidden, pred_weight, mask):
    rows, width = out_weight.shape
    weight = jnp.broadcast_to(out_weight[None], (8, rows, width)).reshape(8 * rows, width)
    weight = lax.all_to_all(weight, ("x", "z"), 0, 0, tiled=True)
    weight = lax.all_gather(weight, ("h", "y"), axis=0, tiled=True)

    packed = lax.all_to_all(pack(queries, keys, values), "y", 0, 0, tiled=True)
    kv_own = packed[:, :2]
    q_own = packed[:, 2]
    kvs = [kv_own] + [lax.ppermute(kv_own, "x", ring(4, d)) for d in (2, 1, 3)]
    q_far = lax.ppermute(q_own, "z", ring(2, 1))

    flat_hidden = pred_hidden.reshape(-1, pred_hidden.shape[2])
    pred = jnp.dot(flat_hidden, pred_weight, preferred_element_type=jnp.float32)
    hidden_rows = flat_hidden.T.reshape(8, 8, -1, flat_hidden.shape[0])
    hidden_rows = hidden_rows.transpose(1, 0, 2, 3).reshape(-1, flat_hidden.shape[0])

    here = lax.axis_index("z").astype(jnp.int32).reshape(1)
    parts = attend(here, q_own, q_far, kvs)
    parts = lax.all_to_all(parts, ("y", "z"), 0, 0, tiled=True)
    attended = lax.all_gather(combine(parts), TENSOR, axis=0)

    summed, stats = project(attended, weight, residual)
    stats = lax.all_gather(stats, TENSOR, axis=0)
    target, product = finish(stats, summed, pred, hidden_rows, mask)

    product = lax.all_to_all(product.reshape(8, -1, width), ("x", "z"), 0, 0, tiled=True)
    product = jnp.sum(product.astype(jnp.float32), axis=0).astype(jnp.bfloat16)
    product = lax.all_to_all(product.reshape(8, -1, width), ("h", "y"), 0, 0, tiled=True)
    grad_scale = 1.0 / math.sqrt(MASKS * CLIPS * MASKED)
    pred_grad = jnp.sum(product.astype(jnp.float32), axis=0) * grad_scale
    return (target, pred_grad)


def solution(mesh):
    fine = Mesh(mesh.devices.reshape(2, 4, 4, 2, 4, 2), SEQ + TENSOR)
    placed = (
        P(SEQ, TENSOR),
        P(SEQ, TENSOR),
        P(SEQ, TENSOR),
        P(SEQ, TENSOR),
        P(SEQ, TENSOR),
        P(None, SEQ, None),
        P(None, TENSOR),
        P(None, SEQ),
    )
    return jax.shard_map(
        body,
        mesh=fine,
        in_specs=placed,
        out_specs=(P(SEQ, TENSOR), P(SEQ, TENSOR)),
        check_vma=False,
    )
```

time: 219 us -> 171 us (0.78)
  the two profiles are of different devices: /device:TPU:8 before, /device:TPU:2 now
where the time goes in v2:
time: 171 us; the launch traced here: 170 us
  blocking collectives  107 us (63%)
  starting transfers between devices  16.5 us (10%)
  waiting for transfers between devices  15.6 us (9%)
  between operations  14.1 us (8%)
  Pallas kernels  11.3 us (7%)
  local copies, waits for them, and re-layouts  4.51 us (3%)
    all_to_all x1, blocking collectives, body(): lax.all_to_all(product.reshape(8, -1, width), ('x', 'z'), 0, 0, tiled=True)  24.8 us
    all_gather x1, blocking collectives, body(): attended = lax.all_gather(combine(parts), TENSOR, axis=0)  22.1 us
    all_to_all x1, blocking collectives, body(): lax.all_to_all(product.reshape(8, -1, width), ('h', 'y'), 0, 0, tiled=True)  17.6 us
    all_to_all x1, blocking collectives, body(): weight = lax.all_to_all(weight, ('x', 'z'), 0, 0, tiled=True)  16.7 us
    all_to_all x1, blocking collectives, body(): packed = lax.all_to_all(pack(queries, keys, values), 'y', 0, 0, tiled=True)  14.2 us
    all_to_all x1, waiting for transfers between devices, body(): parts = lax.all_to_all(parts, ('y', 'z'), 0, 0, tiled=True)  11.8 us
    all_gather x1, blocking collectives, body(): stats = lax.all_gather(stats, TENSOR, axis=0)  11.5 us
    ppermute x3, starting transfers between devices, body(): kvs = [kv_own] + [lax.ppermute(kv_own, 'x', ring(4, d)) for d in (2, 1, 3)]  9.3 us
  transfers between devices with their start and end apart: 6, of which 2 were waited for; matrix products, arithmetic and copies ran while one was open for 1% of the time, Pallas kernels for 5%

profile of v2, /device:TPU:2, one launch (start us, length us, event | category | flops | bytes accessed | tf_op | source)
XLA Modules:
  0.0 170.5 jit_solution(3357840092052768335)
XLA Ops:
  7.2 0.0 copy-start
  7.2 0.0 all-gather.5.cloned.1.call-start
  7.2 1.0 broadcast_in_dim.2
  8.3 16.7 %all_to_all.29 = bf16[8,48,768]{2,1,0:T(8,128)(2,1)} all-to-all(bf16[8,48,768]{2,1,0:T(8,128)(2,1)S(1)} %broadcast_in_dim.2), channel_id=1, replica_groups=mesh['h'=2,'y'=4,'x'=4,'z'=2,'w'=4,'c'=2] {'x','z'}, dimensions={0} | all-to-all | bytes 1179648 | tf_op jit(solution)/shard_map/all_to_all | solution.py:230
  25.0 0.0 all-gather.5.cloned.1.call-update
  25.0 1.8 %shard_map.95 = bf16[4,3,128,128]{3,2,1,0:T(8,128)(2,1)} custom-call(bf16[128,384]{1,0:T(8,128)(2,1)} %queries.1, bf16[128,384]{1,0:T(8,128)(2,1)} %keys.1, bf16[128,384]{1,0:T(8,128)(2,1)} %values.1), custom_call_target="tpu_custom_call" | custom-call | tf_op jit(solution)/shard_map/pallas_call | solution.py:54
  26.8 14.2 %all_to_all.30 = bf16[4,3,128,128]{3,2,1,0:T(8,128)(2,1)S(1)} all-to-all(bf16[4,3,128,128]{3,2,1,0:T(8,128)(2,1)} %shard_map.95), channel_id=1, replica_groups=mesh['h'=2,'y'=4,'x'=4,'z'=2,'w'=4,'c'=2] {'y'}, dimensions={0} | all-to-all | bytes 786432 | tf_op jit(solution)/shard_map/all_to_all | solution.py:233
  41.1 3.5 %collective-permute-start.1 = (bf16[4,2,128,128]{3,2,1,0:T(8,128)(2,1)S(1)}, bf16[4,2,128,128]{3,2,1,0:T(8,128)(2,1)S(1)}, u32[]{:S(2)}, u32[]{:S(2)}) collective-permute-start(bf16[4,2,128,128]{3,2,1,0:T(8,128)(2,1)S(1)} %slice.9.kv0), channel_id=1, source_target_pairs={{0,32},{16,48},{32,0},{48,16},{1,33},{17,49},{33,1},{49,17},{2,34}... | collective-permute-start | bytes 786440 | tf_op jit(solution)/shard_map/ppermute | solution.py:236
  44.5 3.4 %collective-permute-start.2 = (bf16[4,2,128,128]{3,2,1,0:T(8,128)(2,1)S(1)}, bf16[4,2,128,128]{3,2,1,0:T(8,128)(2,1)S(1)}, u32[]{:S(2)}, u32[]{:S(2)}) collective-permute-start(bf16[4,2,128,128]{3,2,1,0:T(8,128)(2,1)S(1)} %slice.9.kv0), channel_id=1, source_target_pairs={{0,16},{16,32},{32,48},{48,0},{1,17},{17,33},{33,49},{49,1},{2,18}... | collective-permute-start | bytes 786440 | tf_op jit(solution)/shard_map/ppermute | solution.py:236
  48.0 2.4 %collective-permute-start.3 = (bf16[4,2,128,128]{3,2,1,0:T(8,128)(2,1)S(1)}, bf16[4,2,128,128]{3,2,1,0:T(8,128)(2,1)S(1)}, u32[]{:S(2)}, u32[]{:S(2)}) collective-permute-start(bf16[4,2,128,128]{3,2,1,0:T(8,128)(2,1)S(1)} %slice.9.kv0), channel_id=1, source_target_pairs={{0,48},{16,0},{32,16},{48,32},{1,49},{17,1},{33,17},{49,33},{2,50}... | collective-permute-start | bytes 786440 | tf_op jit(solution)/shard_map/ppermute | solution.py:236
  50.4 3.0 %collective-permute-start = (bf16[4,128,128]{2,1,0:T(8,128)(2,1)S(1)}, bf16[4,128,128]{2,1,0:T(8,128)(2,1)S(1)}, u32[]{:S(2)}, u32[]{:S(2)}) collective-permute-start(bf16[4,128,128]{2,1,0:T(8,128)(2,1)S(1)} %slice_bitcast_fusion.q_own), channel_id=1, source_target_pairs={{0,8},{8,0},{1,9},{9,1},{2,10},{10,2},{3,11},{11,3},{4,12},{12,4},... | collective-permute-start | bytes 393224 | tf_op jit(solution)/shard_map/ppermute | solution.py:237
  53.4 3.8 %collective-permute-done.q_far = bf16[4,128,128]{2,1,0:T(8,128)(2,1)S(1)} collective-permute-done((bf16[4,128,128]{2,1,0:T(8,128)(2,1)S(1)}, bf16[4,128,128]{2,1,0:T(8,128)(2,1)S(1)}, u32[]{:S(2)}, u32[]{:S(2)}) %collective-permute-start) | collective-permute-done | bytes 131104 | tf_op jit(solution)/shard_map/ppermute | solution.py:237
  57.3 0.0 collective-permute-done.1.kv1
  57.3 0.0 collective-permute-done.2.kv2
  57.3 0.0 collective-permute-done.3.kv3
  57.3 0.0 copy-start.5
  57.3 4.1 %shard_map.96 = bf16[8,144,128]{2,1,0:T(8,128)(2,1)} custom-call(s32[1]{0:T(128)} %bitcast.here, bf16[4,128,128]{2,1,0:T(8,128)(2,1)S(1)} %slice_bitcast_fusion.q_own, bf16[4,128,128]{2,1,0:T(8,128)(2,1)S(1)} %collective-permute-done.q_far, bf16[4,2,128,128]{3,2,1,0:T(8,128)(2,1)S(1)} %slice.9.kv0, bf16[4,2,128,128]{3,2,1,0:T(8,128)(2,1)S(1)} %collective-permute-done.1.kv1, ...), custom_call_target="tpu_custom_call" | custom-call | flops 1073741824 | bytes 2097152 | tf_op jit(solution)/shard_map/pallas_call | solution.py:96
  61.4 0.0 copy-start.6
  61.4 4.2 %all-to-all-start.1 = ((bf16[8,144,128]{2,1,0:T(8,128)(2,1)}), bf16[8,144,128]{2,1,0:T(8,128)(2,1)}, u32[]{:S(2)}, u32[]{:S(2)}) async-start(bf16[8,144,128]{2,1,0:T(8,128)(2,1)} %shard_map.96), calls=%async_computation.1 | async-start | bytes 589824 | tf_op jit(solution)/shard_map/all_to_all | solution.py:246
  65.6 0.0 copy-done.5
  65.6 0.2 copy.16
  65.8 0.9 copy.15
  66.7 0.0 copy-done
  66.7 0.0 copy-done.6
  66.7 0.0 copy-start.3
  66.7 0.6 fusion.pred
  67.3 11.8 %all-to-all-done.1.chunks = bf16[8,144,128]{2,1,0:T(8,128)(2,1)} async-done(((bf16[8,144,128]{2,1,0:T(8,128)(2,1)}), bf16[8,144,128]{2,1,0:T(8,128)(2,1)}, u32[]{:S(2)}, u32[]{:S(2)}) %all-to-all-start.1) | async-done | bytes 294944 | tf_op jit(solution)/shard_map/all_to_all | solution.py:246
  79.0 1.8 %shard_map.97 = bf16[128,384]{1,0:T(8,128)(2,1)} custom-call(bf16[8,144,128]{2,1,0:T(8,128)(2,1)} %all-to-all-done.1.chunks), custom_call_target="tpu_custom_call" | custom-call | tf_op jit(solution)/shard_map/pallas_call | solution.py:125
  80.8 22.1 %all-gather = bf16[1024,384]{1,0:T(8,128)(2,1)S(1)} all-gather(bf16[128,384]{1,0:T(8,128)(2,1)} %shard_map.97), channel_id=2, replica_groups=mesh['h'=2,'y'=4,'x'=4,'z'=2,'w'=4,'c'=2] {'w','c'}, dimensions={0}, use_global_device_ids=true | all-gather | bytes 884736 | tf_op jit(solution)/shard_map/all_gather | solution.py:247
  103.0 0.0 all-gather.5.cloned.1.call-done.weight
  103.0 0.0 copy-done.3
  103.0 0.0 copy-start.1
  103.0 2.3 %copy-done.1 = bf16[3072,768]{1,0:T(8,128)(2,1)S(1)} copy-done((bf16[3072,768]{1,0:T(8,128)(2,1)S(1)}, bf16[3072,768]{1,0:T(8,128)(2,1)}, u32[]{:S(2)}) %copy-start.1) | copy-done | bytes 4718616
  105.3 0.0 copy-start.2
  105.3 0.0 copy-start.4
  105.3 2.7 %shard_map.98 = (f32[128,768]{1,0:T(8,128)S(1)}, f32[2,128]{1,0:T(2,128)S(1)}) custom-call(bf16[8,128,384]{2,1,0:T(8,128)(2,1)S(1)} %bitcast.17, bf16[3072,768]{1,0:T(8,128)(2,1)S(1)} %copy-done.1, bf16[128,768]{1,0:T(8,128)(2,1)S(1)} %copy-done.3), custom_call_target="tpu_custom_call" | custom-call | flops 603979776 | bytes 4718592 | tf_op jit(solution)/shard_map/pallas_call | solution.py:158
  108.0 11.5 %all-gather.2.stats = f32[8,2,128]{2,1,0:T(2,128)S(1)} all-gather(f32[1,2,128]{2,1,0:T(2,128)S(1)} %bitcast.20), channel_id=3, replica_groups=mesh['h'=2,'y'=4,'x'=4,'z'=2,'w'=4,'c'=2] {'w','c'}, dimensions={0}, use_global_device_ids=true | all-gather | bytes 9216 | tf_op jit(solution)/shard_map/all_gather | solution.py:250
  119.5 0.0 copy-done.2
  119.5 0.0 copy-done.4
  119.5 0.8 shard_map.99
  120.3 24.8 %all_to_all.31 = bf16[8,128,768]{2,1,0:T(8,128)(2,1)S(1)} all-to-all(bf16[8,128,768]{2,1,0:T(8,128)(2,1)S(1)} %bitcast.19), channel_id=1, replica_groups=mesh['h'=2,'y'=4,'x'=4,'z'=2,'w'=4,'c'=2] {'x','z'}, dimensions={0} | all-to-all | bytes 3145728 | tf_op jit(solution)/shard_map/all_to_all | solution.py:253
  145.1 0.2 reduce_sum.21
  145.3 17.6 %all_to_all.32 = bf16[8,16,768]{2,1,0:T(8,128)(2,1)S(1)} all-to-all(bf16[8,16,768]{2,1,0:T(8,128)(2,1)S(1)} %bitcast.25), channel_id=1, replica_groups=mesh['h'=2,'y'=4,'x'=4,'z'=2,'w'=4,'c'=2] {'h','y'}, dimensions={0} | all-to-all | bytes 393216 | tf_op jit(solution)/shard_map/all_to_all | solution.py:255
  163.0 0.6 broadcast_multiply_fusion
  (3 shorter events, 0.1 us)
Async XLA Ops:
  7.2 59.5 %copy-start = (bf16[1024,768]{1,0:T(8,128)(2,1)S(1)}, bf16[1024,768]{1,0:T(8,128)(2,1)}, u32[]{:S(2)}) copy-start(bf16[1024,768]{1,0:T(8,128)(2,1)} %param.14) | copy-start | bytes 4718596
  7.2 95.8 %all-gather.5.cloned.1.call-start = ((), (), s32[]{:S(2)}) async-start(), calls=%async_computation.5 | async-start | bytes 5308416 | tf_op jit(solution)/shard_map/all_gather | solution.py:231
  41.1 16.2 %collective-permute-start.1 = (bf16[4,2,128,128]{3,2,1,0:T(8,128)(2,1)S(1)}, bf16[4,2,128,128]{3,2,1,0:T(8,128)(2,1)S(1)}, u32[]{:S(2)}, u32[]{:S(2)}) collective-permute-start(bf16[4,2,128,128]{3,2,1,0:T(8,128)(2,1)S(1)} %slice.9.kv0), channel_id=1, source_target_pairs={{0,32},{16,48},{32,0},{48,16},{1,33},{17,49},{33,1},{49,17},{2,34}... | collective-permute-start | bytes 786440 | tf_op jit(solution)/shard_map/ppermute | solution.py:236
  44.5 12.7 %collective-permute-start.2 = (bf16[4,2,128,128]{3,2,1,0:T(8,128)(2,1)S(1)}, bf16[4,2,128,128]{3,2,1,0:T(8,128)(2,1)S(1)}, u32[]{:S(2)}, u32[]{:S(2)}) collective-permute-start(bf16[4,2,128,128]{3,2,1,0:T(8,128)(2,1)S(1)} %slice.9.kv0), channel_id=1, source_target_pairs={{0,16},{16,32},{32,48},{48,0},{1,17},{17,33},{33,49},{49,1},{2,18}... | collective-permute-start | bytes 786440 | tf_op jit(solution)/shard_map/ppermute | solution.py:236
  48.0 9.3 %collective-permute-start.3 = (bf16[4,2,128,128]{3,2,1,0:T(8,128)(2,1)S(1)}, bf16[4,2,128,128]{3,2,1,0:T(8,128)(2,1)S(1)}, u32[]{:S(2)}, u32[]{:S(2)}) collective-permute-start(bf16[4,2,128,128]{3,2,1,0:T(8,128)(2,1)S(1)} %slice.9.kv0), channel_id=1, source_target_pairs={{0,48},{16,0},{32,16},{48,32},{1,49},{17,1},{33,17},{49,33},{2,50}... | collective-permute-start | bytes 786440 | tf_op jit(solution)/shard_map/ppermute | solution.py:236
  50.4 6.9 %collective-permute-start = (bf16[4,128,128]{2,1,0:T(8,128)(2,1)S(1)}, bf16[4,128,128]{2,1,0:T(8,128)(2,1)S(1)}, u32[]{:S(2)}, u32[]{:S(2)}) collective-permute-start(bf16[4,128,128]{2,1,0:T(8,128)(2,1)S(1)} %slice_bitcast_fusion.q_own), channel_id=1, source_target_pairs={{0,8},{8,0},{1,9},{9,1},{2,10},{10,2},{3,11},{11,3},{4,12},{12,4},... | collective-permute-start | bytes 393224 | tf_op jit(solution)/shard_map/ppermute | solution.py:237
  57.3 8.3 %copy-start.5 = (bf16[2,128,1024]{2,1,0:T(8,128)(2,1)S(1)}, bf16[2,128,1024]{2,1,0:T(8,128)(2,1)}, u32[]{:S(2)}) copy-start(bf16[2,128,1024]{2,1,0:T(8,128)(2,1)} %param.13) | copy-start | bytes 1572868
  61.4 5.3 %copy-start.6 = (bf16[2,128,1024]{2,1,0:T(8,128)(2,1)S(1)}, bf16[2,128,1024]{2,1,0:T(8,128)(2,1)}, u32[]{:S(2)}) copy-start(bf16[2,128,1024]{2,1,0:T(8,128)(2,1)} %param.13) | copy-start | bytes 1572868
  61.4 17.7 %all-to-all-start.1 = ((bf16[8,144,128]{2,1,0:T(8,128)(2,1)}), bf16[8,144,128]{2,1,0:T(8,128)(2,1)}, u32[]{:S(2)}, u32[]{:S(2)}) async-start(bf16[8,144,128]{2,1,0:T(8,128)(2,1)} %shard_map.96), calls=%async_computation.1 | async-start | bytes 589824 | tf_op jit(solution)/shard_map/all_to_all | solution.py:246
  66.7 36.3 %copy-start.3 = (bf16[128,768]{1,0:T(8,128)(2,1)S(1)}, bf16[128,768]{1,0:T(8,128)(2,1)}, u32[]{:S(2)}) copy-start(bf16[128,768]{1,0:T(8,128)(2,1)} %residual.1) | copy-start | bytes 589828
  103.0 2.3 %copy-start.1 = (bf16[3072,768]{1,0:T(8,128)(2,1)S(1)}, bf16[3072,768]{1,0:T(8,128)(2,1)}, u32[]{:S(2)}) copy-start(bf16[3072,768]{1,0:T(8,128)(2,1)} %all-gather.5.cloned.1.call-done.weight) | copy-start | bytes 14155780
  105.3 14.2 %copy-start.2 = (bf16[8,8,16,256]{3,2,1,0:T(8,128)(2,1)S(1)}, bf16[8,8,16,256]{3,2,1,0:T(8,128)(2,1)}, u32[]{:S(2)}) copy-start(bf16[8,8,16,256]{3,2,1,0:T(8,128)(2,1)} %copy.15) | copy-start | bytes 1572868
  105.3 14.2 %copy-start.4 = (s32[2,128]{1,0:T(2,128)S(1)}, s32[2,128]{1,0:T(2,128)}, u32[]{:S(2)}) copy-start(s32[2,128]{1,0:T(2,128)} %mask.1) | copy-start | bytes 3076
Sparse Core Ops, SparseCore 0:
  25.1 67.6 all-gather.4

commit v3 on v2

v3 whole, which is shorter than its diff:
```python
import math

import jax
import jax.numpy as jnp
from jax import lax
from jax.experimental import pallas as pl
from jax.experimental.pallas import tpu as pltpu
from jax.sharding import Mesh
from jax.sharding import PartitionSpec as P

D = 6144
HD = 128
CLIPS = 2
MASKS = 2
MASKED = 3072
HEADS_HERE = 3
SEQ = ("h", "y", "x", "z")
TENSOR = ("w", "c")
LOG2E_ROOT = math.log2(math.e) / math.sqrt(HD)
LEVEL_ROWS = 16
MARK_ROWS = 16
VMEM = pl.BlockSpec(memory_space=pltpu.VMEM)
SMEM = pl.BlockSpec(memory_space=pltpu.SMEM)
ROOMY = pltpu.CompilerParams(vmem_limit_bytes=40 * 1024 * 1024)


def ring(size, distance):
    return [(source, (source + distance) % size) for source in range(size)]


def neighbour(array):
    return lax.ppermute(array, "z", ring(2, 1))


def diagonal(size):
    rows = lax.broadcasted_iota(jnp.int32, (size, size), 0)
    return rows == lax.broadcasted_iota(jnp.int32, (size, size), 1)


def column_to_row(column):
    return jnp.sum(jnp.where(diagonal(column.shape[0]), column, 0.0), axis=0, keepdims=True)


def row_to_column(row):
    return jnp.sum(jnp.where(diagonal(row.shape[1]), row, 0.0), axis=1, keepdims=True)


def pack_kernel(place, queries, keys, values, weight, one, two, three, four, weights):
    for distance, out in enumerate((one, two, three, four)):
        head = jnp.minimum(place[1] ^ distance, HEADS_HERE - 1)
        columns = pl.ds(pl.multiple_of(head * HD, HD), HD)
        out[0] = keys[:, columns]
        out[1] = values[:, columns]
        out[2] = queries[:, columns]
    for copy in range(weights.shape[0]):
        weights[copy] = weight[...]


def pack(place, queries, keys, values, weight):
    piece = jax.ShapeDtypeStruct((3, queries.shape[0], HD), jnp.bfloat16)
    return pl.pallas_call(
        pack_kernel,
        out_shape=(piece,) * 4 + (jax.ShapeDtypeStruct((8,) + weight.shape, jnp.bfloat16),),
        in_specs=[SMEM] + [VMEM] * 4,
        out_specs=(VMEM,) * 5,
    )(place, queries, keys, values, weight)


def attend_kernel(place, q_own, q_far, kv0, kv1, kv2, kv3, out):
    parts = (kv0, kv1, kv2, kv3)
    keys = jnp.concatenate([p[i, 0] for p in parts for i in range(p.shape[0])], axis=0)
    values = jnp.concatenate([p[i, 1] for p in parts for i in range(p.shape[0])], axis=0)
    for q_ref, side in ((q_own, place[0]), (q_far, 1 - place[0])):
        for block in range(0, q_ref.shape[0], 2):
            query = jnp.concatenate([q_ref[block], q_ref[block + 1]], axis=0)
            scores = lax.dot_general(
                query, keys, (((1,), (1,)), ((), ())), preferred_element_type=jnp.float32
            )
            best = jnp.max(scores, axis=1, keepdims=True)
            exponent = jnp.exp2((scores - best) * LOG2E_ROOT)
            total = jnp.sum(exponent, axis=1, keepdims=True)
            summed = jnp.dot(
                exponent.astype(jnp.bfloat16), values, preferred_element_type=jnp.float32
            )
            summed = (summed / total).astype(jnp.bfloat16)
            level = best * LOG2E_ROOT + jnp.log2(total)
            for half in range(2):
                rows = slice(half * HD, (half + 1) * HD)
                row = column_to_row(level[rows])
                first = row.astype(jnp.bfloat16).astype(jnp.float32)
                second = (row - first).astype(jnp.bfloat16).astype(jnp.float32)
                third = row - first - second
                terms = jnp.concatenate(
                    [first, second, third, jnp.zeros((LEVEL_ROWS - 3, HD), jnp.float32)], axis=0
                )
                chunk = 2 * (place[1] ^ (block + half)) + side
                out[chunk, :HD, :] = summed[rows]
                out[chunk, HD:, :] = terms.astype(jnp.bfloat16)


def attend(place, q_own, q_far, kvs):
    chunks = 2 * q_own.shape[0]
    return pl.pallas_call(
        attend_kernel,
        out_shape=jax.ShapeDtypeStruct((chunks, HD + LEVEL_ROWS, HD), jnp.bfloat16),
        in_specs=[SMEM] + [VMEM] * 6,
        out_specs=VMEM,
        compiler_params=ROOMY,
        cost_estimate=pl.CostEstimate(
            flops=4 * 1024 * 2048 * HD, bytes_accessed=2**21, transcendentals=1024 * 2048
        ),
    )(place, q_own, q_far, *kvs)


def combine_kernel(place, chunks, kept, sent):
    heads = []
    for head in range(HEADS_HERE):
        levels = []
        for part in range(2):
            terms = chunks[2 * head + part, HD:, :].astype(jnp.float32)
            levels.append(row_to_column(terms[0:1] + terms[1:2] + terms[2:3]))
        best = jnp.maximum(levels[0], levels[1])
        weights = [jnp.exp2(level - best) for level in levels]
        summed = sum(
            weights[part] * chunks[2 * head + part, :HD, :].astype(jnp.float32) for part in range(2)
        )
        heads.append(summed / (weights[0] + weights[1]))
    columns = jnp.concatenate(heads, axis=1)
    halves = []
    for z in range(2):
        blocks = [columns[:, 96 * x + 48 * z : 96 * x + 48 * z + 48] for x in range(4)]
        half = None
        for x in range(4):
            turned = jnp.concatenate(blocks[x:] + blocks[:x], axis=1)
            half = turned if half is None else jnp.where(place[2] == x, turned, half)
        halves.append(half)
    first = place[0] == 0
    kept[...] = jnp.where(first, halves[0], halves[1]).astype(jnp.bfloat16)
    sent[...] = jnp.where(first, halves[1], halves[0]).astype(jnp.bfloat16)


def combine(place, chunks):
    shape = jax.ShapeDtypeStruct((HD, HEADS_HERE * HD // 2), jnp.bfloat16)
    return pl.pallas_call(
        combine_kernel,
        out_shape=(shape, shape),
        in_specs=[SMEM, VMEM],
        out_specs=(VMEM, VMEM),
    )(place, chunks)


def project_kernel(columns, residual, mask, one, two, three, four, partial, sent):
    pieces, tokens, width = columns.shape
    half = width // 2
    total = jnp.concatenate([residual[...].astype(jnp.float32), jnp.zeros(residual.shape, jnp.float32)], axis=0)
    for piece in range(pieces):
        left = jnp.concatenate([columns[piece, :, :half], columns[piece, :, half:]], axis=0)
        right = jnp.concatenate([ref[piece] for ref in (one, two, three, four)], axis=0)
        total += jnp.dot(left, right, preferred_element_type=jnp.float32)
    partial[...] = total
    sent[: 2 * tokens, :] = total.astype(jnp.bfloat16)
    marks = mask[...].astype(jnp.float32)
    marks = jnp.concatenate([marks, jnp.zeros((sent.shape[0] - 2 * tokens - MASKS, tokens), jnp.float32)], axis=0)
    sent[2 * tokens :, :] = jnp.concatenate([marks] * (sent.shape[1] // tokens), axis=1).astype(jnp.bfloat16)


def project(columns, residual, mask, weights):
    pieces, tokens, _ = columns.shape
    rows, width = weights[0].shape[1:]
    count = 4 * pieces * rows * width
    return pl.pallas_call(
        project_kernel,
        out_shape=(
            jax.ShapeDtypeStruct((2 * tokens, width), jnp.float32),
            jax.ShapeDtypeStruct((2 * tokens + MARK_ROWS, width), jnp.bfloat16),
        ),
        in_specs=[VMEM] * 7,
        out_specs=(VMEM, VMEM),
        compiler_params=ROOMY,
        cost_estimate=pl.CostEstimate(
            flops=4 * tokens * count, bytes_accessed=2 * count, transcendentals=0
        ),
    )(columns, residual, mask, *weights)


def add_kernel(partial, arrived, summed, stats):
    tokens = partial.shape[0] // 2
    for side in range(2):
        rows = slice(side * tokens, (side + 1) * tokens)
        other = slice((1 - side) * tokens, (2 - side) * tokens)
        total = partial[rows, :] + arrived[other, :].astype(jnp.float32)
        summed[rows, :] = total
        mean = jnp.sum(total, axis=1, keepdims=True) / total.shape[1]
        off = total - mean
        stats[0:1, rows] = column_to_row(mean)
        stats[1:2, rows] = column_to_row(jnp.sum(off * off, axis=1, keepdims=True))


def add_up(partial, arrived):
    rows, width = partial.shape
    return pl.pallas_call(
        add_kernel,
        out_shape=(
            jax.ShapeDtypeStruct((rows, width), jnp.float32),
            jax.ShapeDtypeStruct((2, rows), jnp.float32),
        ),
        in_specs=[VMEM] * 2,
        out_specs=(VMEM, VMEM),
        compiler_params=ROOMY,
    )(partial, arrived)


def finish_kernel(stats, summed, arrived, mask, pred, pred_far, hidden, target, product):
    rows_here, width = summed.shape
    tokens = rows_here // 2
    errors = []
    for side, prediction in enumerate((pred, pred_far)):
        rows = slice(side * tokens, (side + 1) * tokens)
        means = stats[:, 0, rows]
        mean = jnp.sum(means, axis=0, keepdims=True) * (width / D)
        shift = means - mean
        var = jnp.sum(stats[:, 1, rows] + width * shift * shift, axis=0, keepdims=True) / D
        scale = row_to_column(lax.rsqrt(var + 1e-06))
        value = ((summed[rows, :] - row_to_column(mean)) * scale).astype(jnp.bfloat16)
        if side == 0:
            target[...] = value
        value = value.astype(jnp.float32)
        for k in range(MASKS):
            if side == 0:
                marks = mask[k : k + 1, :].astype(jnp.float32)
            else:
                marks = arrived[rows_here + k : rows_here + k + 1, :tokens].astype(jnp.float32)
            difference = jnp.clip(prediction[k * tokens : (k + 1) * tokens, :] - value, -1.0, 1.0)
            errors.append((difference * row_to_column(marks)).astype(jnp.bfloat16))
    error = jnp.concatenate(errors, axis=0)
    step = 256
    for start in range(0, hidden.shape[0], step):
        product[start : start + step, :] = jnp.dot(
            hidden[start : start + step, :], error, preferred_element_type=jnp.float32
        ).astype(jnp.bfloat16)


def finish(stats, summed, arrived, mask, pred, pred_far, hidden):
    rows, width = summed.shape
    return pl.pallas_call(
        finish_kernel,
        out_shape=(
            jax.ShapeDtypeStruct((rows // 2, width), jnp.bfloat16),
            jax.ShapeDtypeStruct((hidden.shape[0], width), jnp.bfloat16),
        ),
        in_specs=[VMEM] * 7,
        out_specs=(VMEM, VMEM),
        compiler_params=ROOMY,
        cost_estimate=pl.CostEstimate(
            flops=2 * hidden.shape[0] * hidden.shape[1] * width,
            bytes_accessed=2**22,
            transcendentals=0,
        ),
    )(stats, summed, arrived, mask, pred, pred_far, hidden)


def body(queries, keys, values, residual, out_weight, pred_hidden, pred_weight, mask):
    place = jnp.stack(
        [lax.axis_index(name) for name in ("z", "y", "x")]
    ).astype(jnp.int32)
    *pieces, weight = pack(place, queries, keys, values, out_weight)
    for distance in (1, 2, 3):
        pairs = [(i, i ^ distance) for i in range(4) if i ^ distance < HEADS_HERE]
        pieces[distance] = lax.ppermute(pieces[distance], "y", pairs)
    pieces[1], weight = lax.optimization_barrier((pieces[1], weight))
    kv_own = jnp.stack([piece[:2] for piece in pieces])
    q_own = jnp.stack([piece[2] for piece in pieces])

    width = out_weight.shape[1]
    weight = lax.all_to_all(weight, ("h", "y"), 0, 0, tiled=True)

    kvs = [kv_own] + [lax.ppermute(kv_own, "x", ring(4, d)) for d in (2, 1, 3)]
    q_far = neighbour(q_own)
    kvs, q_far, weight = lax.optimization_barrier((kvs, q_far, weight))
    parts = attend(place, q_own, q_far, kvs)

    hidden = pred_hidden.reshape(-1, pred_hidden.shape[2])
    hidden_far = neighbour(hidden)

    def predict(states):
        return jnp.dot(states, pred_weight, preferred_element_type=jnp.float32)

    hidden_own, parts = lax.optimization_barrier((hidden, parts))
    pred = predict(hidden_own)
    weight, pred = lax.optimization_barrier((weight, pred))
    weights = [weight] + [lax.ppermute(weight, "x", ring(4, -d)) for d in (1, 2, 3)]

    parts = lax.all_to_all(parts, ("y", "z"), 0, 0, tiled=True)
    parts, hidden_far = lax.optimization_barrier((parts, hidden_far))
    kept, sent = combine(place, parts)
    attended = jnp.concatenate((kept, neighbour(sent)), axis=1)
    attended = lax.all_gather(attended, "w", axis=0)
    attended = lax.all_gather(attended, "c", axis=1).reshape((8,) + attended.shape[1:])

    partial, sent = project(attended, residual, mask, weights)
    arrived = neighbour(sent)
    hidden, hidden_far, sent = lax.optimization_barrier((hidden, hidden_far, sent))
    pred_far = predict(hidden_far)
    z = lax.axis_index("z")
    hidden_rows = [
        lax.dynamic_index_in_dim(h.T.reshape(8, 4, 2, 16, -1), z, 2, keepdims=False)
        for h in (hidden, hidden_far)
    ]
    hidden_rows = jnp.concatenate(hidden_rows, axis=3).transpose(1, 0, 2, 3)
    hidden_rows = hidden_rows.reshape(-1, 2 * hidden.shape[0])

    summed, stats = add_up(partial, arrived)
    stats = lax.all_gather(stats, TENSOR, axis=0)
    target, product = finish(stats, summed, arrived, mask, pred, pred_far, hidden_rows)

    product = lax.all_to_all(product.reshape(4, -1, width), "x", 0, 0, tiled=True)
    product = jnp.sum(product.astype(jnp.float32), axis=0).astype(jnp.bfloat16)
    product = lax.all_to_all(product.reshape(8, -1, width), ("h", "y"), 0, 0, tiled=True)
    grad_scale = 1.0 / math.sqrt(MASKS * CLIPS * MASKED)
    pred_grad = jnp.sum(product.astype(jnp.float32), axis=0) * grad_scale
    return (target, pred_grad)


def solution(mesh):
    fine = Mesh(mesh.devices.reshape(2, 4, 4, 2, 4, 2), SEQ + TENSOR)
    placed = (
        P(SEQ, TENSOR),
        P(SEQ, TENSOR),
        P(SEQ, TENSOR),
        P(SEQ, TENSOR),
        P(SEQ, TENSOR),
        P(None, SEQ, None),
        P(None, TENSOR),
        P(None, SEQ),
    )
    return jax.shard_map(
        body,
        mesh=fine,
        in_specs=placed,
        out_specs=(P(SEQ, TENSOR), P(SEQ, TENSOR)),
        check_vma=False,
    )
```

time: 171 us -> 159 us (0.930)
  starting transfers between devices: 16.5 us -> 56.7 us
  blocking collectives: 107 us -> 67.3 us
  between operations: 14.1 us -> 0.98 us
  waiting for transfers between devices: 15.6 us -> 9.7 us
  matrix products: 0.57 us -> 3.3 us
    all_to_all x3 -> x1, blocking collectives: 55.7 us -> 16 us  [body(): lax.all_to_all(product.reshape(4, -1, width), 'x', 0, 0, tiled=True)]
    ppermute x1 -> x10, starting transfers between devices: 3.01 us -> 30.6 us  [the longest x4 14.9 us: neighbour(): return lax.ppermute(array, 'z', ring(2, 1))]
    all_to_all x1, waiting for transfers between devices: 11.8 us -> 0.01 us  [body(): parts = lax.all_to_all(parts, ('y', 'z'), 0, 0, tiled=True)]
    all_to_all x0 -> x1, starting transfers between devices: none -> 8.46 us  [body(): weight = lax.all_to_all(weight, ('h', 'y'), 0, 0, tiled=True)]
    ppermute x1 -> x10, waiting for transfers between devices: 3.84 us -> 9.69 us  [the longest x4 9.68 us: neighbour(): return lax.ppermute(array, 'z', ring(2, 1))]
    all_gather x1, blocking collectives: 11.5 us -> 14.3 us  [body(): stats = lax.all_gather(stats, TENSOR, axis=0)]
    dot_general x1 -> x2, matrix products: 0.57 us -> 3.3 us  [predict(): return jnp.dot(states, pred_weight, preferred_element_type=jnp.float32)]
    all_to_all x1, blocking collectives: 17.6 us -> 15.2 us  [body(): lax.all_to_all(product.reshape(8, -1, width), ('h', 'y'), 0, 0, tiled=True)]
  transfers between devices with their start and end apart: 6 -> 15, of which waited for: 2 -> 2; matrix products, arithmetic and copies ran while one was open for 1% -> 6% of each run, Pallas kernels for 5% -> 4%
where the time goes in v3:
time: 159 us; the launch traced here: 158 us
  blocking collectives  67.3 us (42%)
  starting transfers between devices  56.7 us (36%)
  Pallas kernels  12.7 us (8%)
  waiting for transfers between devices  9.7 us (6%)
  local copies, waits for them, and re-layouts  4.79 us (3%)
  matrix products  3.3 us (2%)
  other arithmetic  2.41 us (2%)
    all_gather x1, blocking collectives, body(): attended = lax.all_gather(attended, 'w', axis=0)  19.4 us
    all_to_all x1, blocking collectives, body(): lax.all_to_all(product.reshape(4, -1, width), 'x', 0, 0, tiled=True)  16 us
    all_to_all x1, blocking collectives, body(): lax.all_to_all(product.reshape(8, -1, width), ('h', 'y'), 0, 0, tiled=True)  15.2 us
    ppermute x4, starting transfers between devices, neighbour(): return lax.ppermute(array, 'z', ring(2, 1))  14.9 us
    all_gather x1, blocking collectives, body(): stats = lax.all_gather(stats, TENSOR, axis=0)  14.3 us
    ppermute x3, starting transfers between devices, body(): kvs = [kv_own] + [lax.ppermute(kv_own, 'x', ring(4, d)) for d in (2, 1, 3)]  11.1 us
    ppermute x4, waiting for transfers between devices, neighbour(): return lax.ppermute(array, 'z', ring(2, 1))  9.68 us
    ppermute x3, starting transfers between devices, body(): lax.ppermute(weight, 'x', ring(4, -d))  8.55 us
  transfers between devices with their start and end apart: 15, of which 2 were waited for; matrix products, arithmetic and copies ran while one was open for 6% of the time, Pallas kernels for 4%

profile of v3, /device:TPU:2, one launch (start us, length us, event | category | flops | bytes accessed | tf_op | source)
XLA Modules:
  0.0 157.8 jit_solution(13330296461597234499)
XLA Ops:
  0.6 0.0 copy-start
  0.7 0.6 pad_add_fusion.place
  1.2 2.1 %shard_map.95 = (bf16[3,128,128]{2,1,0:T(8,128)(2,1)}, bf16[3,128,128]{2,1,0:T(8,128)(2,1)}, bf16[3,128,128]{2,1,0:T(8,128)(2,1)}, bf16[3,128,128]{2,1,0:T(8,128)(2,1)}, bf16[8,48,768]{2,1,0:T(8,128)(2,1)}) custom-call(s32[3]{0:T(128)} %pad_add_fusion.place, bf16[128,384]{1,0:T(8,128)(2,1)} %queries.1, bf16[128,384]{1,0:T(8,128)(2,1)} %keys.1, ...), custom_call_target="tpu_custom_call" | custom-call | tf_op jit(solution)/shard_map/pallas_call | solution.py:61
  3.3 3.5 %collective-permute-start = (bf16[3,128,128]{2,1,0:T(8,128)(2,1)}, bf16[3,128,128]{2,1,0:T(8,128)(2,1)S(1)}, u32[]{:S(2)}, u32[]{:S(2)}) collective-permute-start(bf16[3,128,128]{2,1,0:T(8,128)(2,1)} %get-tuple-element.32), channel_id=1, source_target_pairs={{0,64},{64,0},{192,128},{1,65},{65,1},{193,129},{2,66},{66,2},{194... | collective-permute-start | bytes 294920 | tf_op jit(solution)/shard_map/ppermute | solution.py:269
  6.8 2.3 %collective-permute-start.1 = (bf16[3,128,128]{2,1,0:T(8,128)(2,1)}, bf16[3,128,128]{2,1,0:T(8,128)(2,1)S(1)}, u32[]{:S(2)}, u32[]{:S(2)}) collective-permute-start(bf16[3,128,128]{2,1,0:T(8,128)(2,1)} %get-tuple-element.35), channel_id=1, source_target_pairs={{0,128},{128,0},{192,64},{1,129},{129,1},{193,65},{2,130},{130,2},... | collective-permute-start | bytes 294920 | tf_op jit(solution)/shard_map/ppermute | solution.py:269
  9.1 1.3 collective-permute-start.2
  10.4 0.8 slice_bitcast_fusion.3
  11.2 0.0 collective-permute-done
  11.2 0.0 copy-start.2
  11.2 8.5 %all-to-all-start = ((bf16[8,48,768]{2,1,0:T(8,128)(2,1)}), bf16[8,48,768]{2,1,0:T(8,128)(2,1)S(1)}, u32[]{:S(2)}, u32[]{:S(2)}) async-start(bf16[8,48,768]{2,1,0:T(8,128)(2,1)} %get-tuple-element.37), calls=%async_computation | async-start | bytes 1179648 | tf_op jit(solution)/shard_map/all_to_all | solution.py:275
  19.7 0.0 collective-permute-done.1
  19.7 0.0 collective-permute-done.2
  19.8 3.8 %collective-permute-start.5 = (bf16[4,2,128,128]{3,2,1,0:T(8,128)(2,1)S(1)}, bf16[4,2,128,128]{3,2,1,0:T(8,128)(2,1)S(1)}, u32[]{:S(2)}, u32[]{:S(2)}) collective-permute-start(bf16[4,2,128,128]{3,2,1,0:T(8,128)(2,1)S(1)} %pad_maximum_fusion.kv0), channel_id=1, source_target_pairs={{0,48},{16,0},{32,16},{48,32},{1,49},{17,1},{33,17},{49,33},{2,50}... | collective-permute-start | bytes 786440 | tf_op jit(solution)/shard_map/ppermute | solution.py:277
  23.6 2.1 %collective-permute-start.4 = (bf16[4,2,128,128]{3,2,1,0:T(8,128)(2,1)S(1)}, bf16[4,2,128,128]{3,2,1,0:T(8,128)(2,1)S(1)}, u32[]{:S(2)}, u32[]{:S(2)}) collective-permute-start(bf16[4,2,128,128]{3,2,1,0:T(8,128)(2,1)S(1)} %pad_maximum_fusion.kv0), channel_id=1, source_target_pairs={{0,16},{16,32},{32,48},{48,0},{1,17},{17,33},{33,49},{49,1},{2,18}... | collective-permute-start | bytes 786440 | tf_op jit(solution)/shard_map/ppermute | solution.py:277
  25.7 5.2 %collective-permute-start.3 = (bf16[4,2,128,128]{3,2,1,0:T(8,128)(2,1)S(1)}, bf16[4,2,128,128]{3,2,1,0:T(8,128)(2,1)S(1)}, u32[]{:S(2)}, u32[]{:S(2)}) collective-permute-start(bf16[4,2,128,128]{3,2,1,0:T(8,128)(2,1)S(1)} %pad_maximum_fusion.kv0), channel_id=1, source_target_pairs={{0,32},{16,48},{32,0},{48,16},{1,33},{17,49},{33,1},{49,17},{2,34}... | collective-permute-start | bytes 786440 | tf_op jit(solution)/shard_map/ppermute | solution.py:277
  30.9 0.8 slice.24
  31.7 4.3 %collective-permute-start.6 = (bf16[4,128,128]{2,1,0:T(8,128)(2,1)S(1)}, bf16[4,128,128]{2,1,0:T(8,128)(2,1)S(1)}, u32[]{:S(2)}, u32[]{:S(2)}) collective-permute-start(bf16[4,128,128]{2,1,0:T(8,128)(2,1)S(1)} %pad_maximum_fusion.1.q_own), channel_id=1, source_target_pairs={{0,8},{8,0},{1,9},{9,1},{2,10},{10,2},{3,11},{11,3},{4,12},{12,4},... | collective-permute-start | bytes 393224 | tf_op jit(solution)/shard_map/ppermute | solution.py:32
  36.0 2.1 %copy.19 = bf16[256,1024]{0,1:T(8,128)(2,1)} copy(bf16[256,1024]{1,0:T(8,128)(2,1)} %bitcast.41) | data formatting | bytes 1048576 | tf_op jit(solution)/shard_map/reshape | solution.py:282
  38.1 1.9 %collective-permute-start.7 = (bf16[256,1024]{0,1:T(8,128)(2,1)}, bf16[256,1024]{0,1:T(8,128)(2,1)}, u32[]{:S(2)}, u32[]{:S(2)}) collective-permute-start(bf16[256,1024]{0,1:T(8,128)(2,1)} %copy.19), channel_id=1, source_target_pairs={{0,8},{8,0},{1,9},{9,1},{2,10},{10,2},{3,11},{11,3},{4,12},{12,4},... | collective-permute-start | bytes 1572872 | tf_op jit(solution)/shard_map/ppermute | solution.py:32
  40.0 0.0 collective-permute-done.6.q_far
  40.0 0.0 collective-permute-done.5.kv3
  40.0 0.0 collective-permute-done.4.kv2
  40.0 0.0 collective-permute-done.3.kv1
  40.0 0.0 all-to-all-done.one
  40.1 0.0 copy-done.2
  40.1 4.7 %shard_map.96 = bf16[8,144,128]{2,1,0:T(8,128)(2,1)} custom-call(s32[3]{0:T(128)S(1)} %copy-done.2, bf16[4,128,128]{2,1,0:T(8,128)(2,1)S(1)} %pad_maximum_fusion.1.q_own, bf16[4,128,128]{2,1,0:T(8,128)(2,1)S(1)} %collective-permute-done.6.q_far, bf16[4,2,128,128]{3,2,1,0:T(8,128)(2,1)S(1)} %pad_maximum_fusion.kv0, ...), custom_call_target="tpu_custom_call" | custom-call | flops 1073741824 | bytes 2097152 | tf_op jit(solution)/shard_map/pallas_call | solution.py:103
  44.8 6.5 %all-to-all-start.1 = ((bf16[8,144,128]{2,1,0:T(8,128)(2,1)}), bf16[8,144,128]{2,1,0:T(8,128)(2,1)}, u32[]{:S(2)}, u32[]{:S(2)}) async-start(bf16[8,144,128]{2,1,0:T(8,128)(2,1)} %shard_map.96), calls=%async_computation.1 | async-start | bytes 589824 | tf_op jit(solution)/shard_map/all_to_all | solution.py:293
  51.3 0.0 copy-done
  51.3 1.6 %fusion.pred = f32[256,768]{1,0:T(8,128)S(1)} fusion(bf16[256,1024]{0,1:T(8,128)(2,1)} %copy.19, bf16[1024,768]{1,0:T(8,128)(2,1)S(1)} %copy-done), kind=kOutput, calls=%fused_computation.13 | convolution fusion | flops 402653184 | bytes 2883584 | tf_op jit(solution)/shard_map/dot_general | solution.py:286
  53.0 0.0 copy-start.3
  53.0 1.9 %collective-permute-start.11 = (bf16[8,48,768]{2,1,0:T(8,128)(2,1)S(1)}, bf16[8,48,768]{2,1,0:T(8,128)(2,1)S(1)}, u32[]{:S(2)}, u32[]{:S(2)}) collective-permute-start(bf16[8,48,768]{2,1,0:T(8,128)(2,1)S(1)} %all-to-all-done.one), channel_id=1, source_target_pairs={{0,16},{16,32},{32,48},{48,0},{1,17},{17,33},{33,49},{49,1},{2,18}... | collective-permute-start | bytes 1769480 | tf_op jit(solution)/shard_map/ppermute | solution.py:291
  54.9 4.4 %collective-permute-start.10 = (bf16[8,48,768]{2,1,0:T(8,128)(2,1)S(1)}, bf16[8,48,768]{2,1,0:T(8,128)(2,1)}, u32[]{:S(2)}, u32[]{:S(2)}) collective-permute-start(bf16[8,48,768]{2,1,0:T(8,128)(2,1)S(1)} %all-to-all-done.one), channel_id=1, source_target_pairs={{0,32},{16,48},{32,0},{48,16},{1,33},{17,49},{33,1},{49,17},{2,34}... | collective-permute-start | bytes 1769480 | tf_op jit(solution)/shard_map/ppermute | solution.py:291
  59.3 2.3 %collective-permute-start.9 = (bf16[8,48,768]{2,1,0:T(8,128)(2,1)S(1)}, bf16[8,48,768]{2,1,0:T(8,128)(2,1)}, u32[]{:S(2)}, u32[]{:S(2)}) collective-permute-start(bf16[8,48,768]{2,1,0:T(8,128)(2,1)S(1)} %all-to-all-done.one), channel_id=1, source_target_pairs={{0,48},{16,0},{32,16},{48,32},{1,49},{17,1},{33,17},{49,33},{2,50}... | collective-permute-start | bytes 1769480 | tf_op jit(solution)/shard_map/ppermute | solution.py:291
  61.6 0.0 collective-permute-done.7
  61.6 0.0 all-to-all-done.1.chunks
  61.6 2.0 %shard_map.97 = (bf16[128,192]{1,0:T(8,128)(2,1)}, bf16[128,192]{1,0:T(8,128)(2,1)}) custom-call(s32[3]{0:T(128)} %pad_add_fusion.place, bf16[8,144,128]{2,1,0:T(8,128)(2,1)} %all-to-all-done.1.chunks), custom_call_target="tpu_custom_call" | custom-call | tf_op jit(solution)/shard_map/pallas_call | solution.py:144
  63.6 3.9 %collective-permute-start.8 = (bf16[128,192]{1,0:T(8,128)(2,1)}, bf16[128,192]{1,0:T(8,128)(2,1)}, u32[]{:S(2)}, u32[]{:S(2)}) collective-permute-start(bf16[128,192]{1,0:T(8,128)(2,1)} %get-tuple-element.46), channel_id=1, source_target_pairs={{0,8},{8,0},{1,9},{9,1},{2,10},{10,2},{3,11},{11,3},{4,12},{12,4},... | collective-permute-start | bytes 147464 | tf_op jit(solution)/shard_map/ppermute | solution.py:32
  67.6 0.0 copy-start.1
  67.6 2.5 %collective-permute-done.8 = bf16[128,192]{1,0:T(8,128)(2,1)} collective-permute-done((bf16[128,192]{1,0:T(8,128)(2,1)}, bf16[128,192]{1,0:T(8,128)(2,1)}, u32[]{:S(2)}, u32[]{:S(2)}) %collective-permute-start.8) | collective-permute-done | bytes 49184 | tf_op jit(solution)/shard_map/ppermute | solution.py:32
  70.1 1.0 pad_maximum_fusion.2
  71.1 19.4 %all-gather = bf16[512,384]{1,0:T(8,128)(2,1)S(1)} all-gather(bf16[128,384]{1,0:T(8,128)(2,1)S(1)} %pad_maximum_fusion.2), channel_id=2, replica_groups=mesh['h'=2,'y'=4,'x'=4,'z'=2,'w'=4,'c'=2] {'w'}, dimensions={0}, use_global_device_ids=true | all-gather | bytes 491520 | tf_op jit(solution)/shard_map/all_gather | solution.py:297
  90.5 2.4 %all-gather.1 = bf16[4,256,384]{2,1,0:T(8,128)(2,1)S(1)} all-gather(bf16[4,128,384]{2,1,0:T(8,128)(2,1)S(1)} %bitcast.39), channel_id=3, replica_groups=mesh['h'=2,'y'=4,'x'=4,'z'=2,'w'=4,'c'=2] {'c'}, dimensions={1}, use_global_device_ids=true | all-gather | bytes 1179648 | tf_op jit(solution)/shard_map/all_gather | solution.py:298
  92.8 0.0 collective-permute-done.11.four
  92.8 0.0 collective-permute-done.10.three
  92.8 0.0 collective-permute-done.9.two
  92.8 0.0 copy-done.3
  92.9 0.0 copy-done.1
  92.9 0.0 copy-start.4
  92.9 2.3 %shard_map.98 = (f32[256,768]{1,0:T(8,128)S(1)}, bf16[272,768]{1,0:T(8,128)(2,1)S(1)}) custom-call(bf16[8,128,384]{2,1,0:T(8,128)(2,1)S(1)} %bitcast.34, bf16[128,768]{1,0:T(8,128)(2,1)S(1)} %copy-done.1, s32[2,128]{1,0:T(2,128)S(1)} %copy-done.3, bf16[8,48,768]{2,1,0:T(8,128)(2,1)S(1)} %all-to-all-done.one, bf16[8,48,768]{2,1,0:T(8,128)(2,1)} %collective-permute-done.9.two, ...), custom_call_target="tpu_custom_call" | custom-call | flops 603979776 | bytes 2359296 | tf_op jit(solution)/shard_map/pallas_call | solution.py:171
  95.2 4.8 %collective-permute-start.12 = (bf16[272,768]{1,0:T(8,128)(2,1)S(1)}, bf16[272,768]{1,0:T(8,128)(2,1)S(1)}, u32[]{:S(2)}, u32[]{:S(2)}) collective-permute-start(bf16[272,768]{1,0:T(8,128)(2,1)S(1)} %get-tuple-element.51), channel_id=1, source_target_pairs={{0,8},{8,0},{1,9},{9,1},{2,10},{10,2},{3,11},{11,3},{4,12},{12,4},... | collective-permute-start | bytes 1253384 | tf_op jit(solution)/shard_map/ppermute | solution.py:32
  100.0 0.0 copy-done.4
  100.0 1.0 dynamic-slice_bitcast_fusion
  101.0 0.1 maximum_bitcast_fusion
  101.2 1.6 %fusion.1.pred_far = f32[256,768]{1,0:T(8,128)S(1)} fusion(bf16[256,1024]{0,1:T(8,128)(2,1)} %collective-permute-done.7, bf16[1024,768]{1,0:T(8,128)(2,1)S(1)} %copy-done), kind=kOutput, calls=%fused_computation.14 | convolution fusion | flops 402653184 | bytes 2883584 | tf_op jit(solution)/shard_map/dot_general | solution.py:286
  102.8 7.1 %collective-permute-done.12.arrived = bf16[272,768]{1,0:T(8,128)(2,1)S(1)} collective-permute-done((bf16[272,768]{1,0:T(8,128)(2,1)S(1)}, bf16[272,768]{1,0:T(8,128)(2,1)S(1)}, u32[]{:S(2)}, u32[]{:S(2)}) %collective-permute-start.12) | collective-permute-done | bytes 417824 | tf_op jit(solution)/shard_map/ppermute | solution.py:32
  109.9 0.3 shard_map.99
  110.2 14.3 %all-gather.3.stats = f32[8,2,256]{2,1,0:T(2,128)S(1)} all-gather(f32[1,2,256]{2,1,0:T(2,128)S(1)} %bitcast.37), channel_id=4, replica_groups=mesh['h'=2,'y'=4,'x'=4,'z'=2,'w'=4,'c'=2] {'w','c'}, dimensions={0}, use_global_device_ids=true | all-gather | bytes 18432 | tf_op jit(solution)/shard_map/all_gather | solution.py:313
  124.5 1.4 shard_map.100
  125.9 16.0 %all_to_all.20 = bf16[4,128,768]{2,1,0:T(8,128)(2,1)S(1)} all-to-all(bf16[4,128,768]{2,1,0:T(8,128)(2,1)S(1)} %bitcast.36), channel_id=1, replica_groups=mesh['h'=2,'y'=4,'x'=4,'z'=2,'w'=4,'c'=2] {'x'}, dimensions={0} | all-to-all | bytes 1572864 | tf_op jit(solution)/shard_map/all_to_all | solution.py:316
  141.9 0.1 reduce_sum.21
  142.0 15.2 %all_to_all.21 = bf16[8,16,768]{2,1,0:T(8,128)(2,1)S(1)} all-to-all(bf16[8,16,768]{2,1,0:T(8,128)(2,1)S(1)} %bitcast.40), channel_id=1, replica_groups=mesh['h'=2,'y'=4,'x'=4,'z'=2,'w'=4,'c'=2] {'h','y'}, dimensions={0} | all-to-all | bytes 393216 | tf_op jit(solution)/shard_map/all_to_all | solution.py:318
  157.2 0.6 broadcast_multiply_fusion
  (10 shorter events, 0.2 us)
Async XLA Ops:
  0.6 50.7 %copy-start = (bf16[1024,768]{1,0:T(8,128)(2,1)S(1)}, bf16[1024,768]{1,0:T(8,128)(2,1)}, u32[]{:S(2)}) copy-start(bf16[1024,768]{1,0:T(8,128)(2,1)} %param.14) | copy-start | bytes 4718596
  3.3 7.9 %collective-permute-start = (bf16[3,128,128]{2,1,0:T(8,128)(2,1)}, bf16[3,128,128]{2,1,0:T(8,128)(2,1)S(1)}, u32[]{:S(2)}, u32[]{:S(2)}) collective-permute-start(bf16[3,128,128]{2,1,0:T(8,128)(2,1)} %get-tuple-element.32), channel_id=1, source_target_pairs={{0,64},{64,0},{192,128},{1,65},{65,1},{193,129},{2,66},{66,2},{194... | collective-permute-start | bytes 294920 | tf_op jit(solution)/shard_map/ppermute | solution.py:269
  6.8 12.9 %collective-permute-start.1 = (bf16[3,128,128]{2,1,0:T(8,128)(2,1)}, bf16[3,128,128]{2,1,0:T(8,128)(2,1)S(1)}, u32[]{:S(2)}, u32[]{:S(2)}) collective-permute-start(bf16[3,128,128]{2,1,0:T(8,128)(2,1)} %get-tuple-element.35), channel_id=1, source_target_pairs={{0,128},{128,0},{192,64},{1,129},{129,1},{193,65},{2,130},{130,2},... | collective-permute-start | bytes 294920 | tf_op jit(solution)/shard_map/ppermute | solution.py:269
  9.1 10.7 %collective-permute-start.2 = (bf16[3,128,128]{2,1,0:T(8,128)(2,1)}, bf16[3,128,128]{2,1,0:T(8,128)(2,1)S(1)}, u32[]{:S(2)}, u32[]{:S(2)}) collective-permute-start(bf16[3,128,128]{2,1,0:T(8,128)(2,1)} %get-tuple-element.36), channel_id=1, source_target_pairs={{64,128},{128,64},{192,0},{65,129},{129,65},{193,1},{66,130},{130,... | collective-permute-start | bytes 294920 | tf_op jit(solution)/shard_map/ppermute | solution.py:269
  11.2 28.8 %copy-start.2 = (s32[3]{0:T(128)S(1)}, s32[3]{0:T(128)}, u32[]{:S(2)}) copy-start(s32[3]{0:T(128)} %pad_add_fusion.place) | copy-start | bytes 40
  11.2 28.8 %all-to-all-start = ((bf16[8,48,768]{2,1,0:T(8,128)(2,1)}), bf16[8,48,768]{2,1,0:T(8,128)(2,1)S(1)}, u32[]{:S(2)}, u32[]{:S(2)}) async-start(bf16[8,48,768]{2,1,0:T(8,128)(2,1)} %get-tuple-element.37), calls=%async_computation | async-start | bytes 1179648 | tf_op jit(solution)/shard_map/all_to_all | solution.py:275
  19.8 20.2 %collective-permute-start.5 = (bf16[4,2,128,128]{3,2,1,0:T(8,128)(2,1)S(1)}, bf16[4,2,128,128]{3,2,1,0:T(8,128)(2,1)S(1)}, u32[]{:S(2)}, u32[]{:S(2)}) collective-permute-start(bf16[4,2,128,128]{3,2,1,0:T(8,128)(2,1)S(1)} %pad_maximum_fusion.kv0), channel_id=1, source_target_pairs={{0,48},{16,0},{32,16},{48,32},{1,49},{17,1},{33,17},{49,33},{2,50}... | collective-permute-start | bytes 786440 | tf_op jit(solution)/shard_map/ppermute | solution.py:277
  23.6 16.4 %collective-permute-start.4 = (bf16[4,2,128,128]{3,2,1,0:T(8,128)(2,1)S(1)}, bf16[4,2,128,128]{3,2,1,0:T(8,128)(2,1)S(1)}, u32[]{:S(2)}, u32[]{:S(2)}) collective-permute-start(bf16[4,2,128,128]{3,2,1,0:T(8,128)(2,1)S(1)} %pad_maximum_fusion.kv0), channel_id=1, source_target_pairs={{0,16},{16,32},{32,48},{48,0},{1,17},{17,33},{33,49},{49,1},{2,18}... | collective-permute-start | bytes 786440 | tf_op jit(solution)/shard_map/ppermute | solution.py:277
  25.7 14.4 %collective-permute-start.3 = (bf16[4,2,128,128]{3,2,1,0:T(8,128)(2,1)S(1)}, bf16[4,2,128,128]{3,2,1,0:T(8,128)(2,1)S(1)}, u32[]{:S(2)}, u32[]{:S(2)}) collective-permute-start(bf16[4,2,128,128]{3,2,1,0:T(8,128)(2,1)S(1)} %pad_maximum_fusion.kv0), channel_id=1, source_target_pairs={{0,32},{16,48},{32,0},{48,16},{1,33},{17,49},{33,1},{49,17},{2,34}... | collective-permute-start | bytes 786440 | tf_op jit(solution)/shard_map/ppermute | solution.py:277
  31.7 8.3 %collective-permute-start.6 = (bf16[4,128,128]{2,1,0:T(8,128)(2,1)S(1)}, bf16[4,128,128]{2,1,0:T(8,128)(2,1)S(1)}, u32[]{:S(2)}, u32[]{:S(2)}) collective-permute-start(bf16[4,128,128]{2,1,0:T(8,128)(2,1)S(1)} %pad_maximum_fusion.1.q_own), channel_id=1, source_target_pairs={{0,8},{8,0},{1,9},{9,1},{2,10},{10,2},{3,11},{11,3},{4,12},{12,4},... | collective-permute-start | bytes 393224 | tf_op jit(solution)/shard_map/ppermute | solution.py:32
  38.1 23.5 %collective-permute-start.7 = (bf16[256,1024]{0,1:T(8,128)(2,1)}, bf16[256,1024]{0,1:T(8,128)(2,1)}, u32[]{:S(2)}, u32[]{:S(2)}) collective-permute-start(bf16[256,1024]{0,1:T(8,128)(2,1)} %copy.19), channel_id=1, source_target_pairs={{0,8},{8,0},{1,9},{9,1},{2,10},{10,2},{3,11},{11,3},{4,12},{12,4},... | collective-permute-start | bytes 1572872 | tf_op jit(solution)/shard_map/ppermute | solution.py:32
  44.8 16.8 %all-to-all-start.1 = ((bf16[8,144,128]{2,1,0:T(8,128)(2,1)}), bf16[8,144,128]{2,1,0:T(8,128)(2,1)}, u32[]{:S(2)}, u32[]{:S(2)}) async-start(bf16[8,144,128]{2,1,0:T(8,128)(2,1)} %shard_map.96), calls=%async_computation.1 | async-start | bytes 589824 | tf_op jit(solution)/shard_map/all_to_all | solution.py:293
  53.0 39.9 %copy-start.3 = (s32[2,128]{1,0:T(2,128)S(1)}, s32[2,128]{1,0:T(2,128)}, u32[]{:S(2)}) copy-start(s32[2,128]{1,0:T(2,128)} %mask.3) | copy-start | bytes 3076
  53.0 39.8 %collective-permute-start.11 = (bf16[8,48,768]{2,1,0:T(8,128)(2,1)S(1)}, bf16[8,48,768]{2,1,0:T(8,128)(2,1)S(1)}, u32[]{:S(2)}, u32[]{:S(2)}) collective-permute-start(bf16[8,48,768]{2,1,0:T(8,128)(2,1)S(1)} %all-to-all-done.one), channel_id=1, source_target_pairs={{0,16},{16,32},{32,48},{48,0},{1,17},{17,33},{33,49},{49,1},{2,18}... | collective-permute-start | bytes 1769480 | tf_op jit(solution)/shard_map/ppermute | solution.py:291
  54.9 37.9 %collective-permute-start.10 = (bf16[8,48,768]{2,1,0:T(8,128)(2,1)S(1)}, bf16[8,48,768]{2,1,0:T(8,128)(2,1)}, u32[]{:S(2)}, u32[]{:S(2)}) collective-permute-start(bf16[8,48,768]{2,1,0:T(8,128)(2,1)S(1)} %all-to-all-done.one), channel_id=1, source_target_pairs={{0,32},{16,48},{32,0},{48,16},{1,33},{17,49},{33,1},{49,17},{2,34}... | collective-permute-start | bytes 1769480 | tf_op jit(solution)/shard_map/ppermute | solution.py:291
  59.3 33.5 %collective-permute-start.9 = (bf16[8,48,768]{2,1,0:T(8,128)(2,1)S(1)}, bf16[8,48,768]{2,1,0:T(8,128)(2,1)}, u32[]{:S(2)}, u32[]{:S(2)}) collective-permute-start(bf16[8,48,768]{2,1,0:T(8,128)(2,1)S(1)} %all-to-all-done.one), channel_id=1, source_target_pairs={{0,48},{16,0},{32,16},{48,32},{1,49},{17,1},{33,17},{49,33},{2,50}... | collective-permute-start | bytes 1769480 | tf_op jit(solution)/shard_map/ppermute | solution.py:291
  63.6 6.5 %collective-permute-start.8 = (bf16[128,192]{1,0:T(8,128)(2,1)}, bf16[128,192]{1,0:T(8,128)(2,1)}, u32[]{:S(2)}, u32[]{:S(2)}) collective-permute-start(bf16[128,192]{1,0:T(8,128)(2,1)} %get-tuple-element.46), channel_id=1, source_target_pairs={{0,8},{8,0},{1,9},{9,1},{2,10},{10,2},{3,11},{11,3},{4,12},{12,4},... | collective-permute-start | bytes 147464 | tf_op jit(solution)/shard_map/ppermute | solution.py:32
  67.6 25.3 %copy-start.1 = (bf16[128,768]{1,0:T(8,128)(2,1)S(1)}, bf16[128,768]{1,0:T(8,128)(2,1)}, u32[]{:S(2)}) copy-start(bf16[128,768]{1,0:T(8,128)(2,1)} %residual.1) | copy-start | bytes 589828
  92.9 7.2 %copy-start.4 = (bf16[256,1024]{0,1:T(8,128)(2,1)S(1)}, bf16[256,1024]{0,1:T(8,128)(2,1)}, u32[]{:S(2)}) copy-start(bf16[256,1024]{0,1:T(8,128)(2,1)} %copy.19) | copy-start | bytes 1572868
  95.2 14.8 %collective-permute-start.12 = (bf16[272,768]{1,0:T(8,128)(2,1)S(1)}, bf16[272,768]{1,0:T(8,128)(2,1)S(1)}, u32[]{:S(2)}, u32[]{:S(2)}) collective-permute-start(bf16[272,768]{1,0:T(8,128)(2,1)S(1)} %get-tuple-element.51), channel_id=1, source_target_pairs={{0,8},{8,0},{1,9},{9,1},{2,10},{10,2},{3,11},{11,3},{4,12},{12,4},... | collective-permute-start | bytes 1253384 | tf_op jit(solution)/shard_map/ppermute | solution.py:32

commit v4 on v3

--- a/solution.py
+++ b/solution.py
@@ -149,6 +149,20 @@
     )(place, chunks)
 
 
+def marks_kernel(mask, marks):
+    marks[...] = mask[...].astype(jnp.float32)
+
+
+def as_marks(mask):
+    return pl.pallas_call(
+        marks_kernel,
+        out_shape=jax.ShapeDtypeStruct(mask.shape, jnp.float32),
+        in_specs=[VMEM],
+        out_specs=VMEM,
+        cost_estimate=pl.CostEstimate(flops=2**29, bytes_accessed=2**21, transcendentals=0),
+    )(mask)
+
+
 def project_kernel(columns, residual, mask, one, two, three, four, partial, sent):
     pieces, tokens, width = columns.shape
     half = width // 2
@@ -159,8 +173,7 @@
         total += jnp.dot(left, right, preferred_element_type=jnp.float32)
     partial[...] = total
     sent[: 2 * tokens, :] = total.astype(jnp.bfloat16)
-    marks = mask[...].astype(jnp.float32)
-    marks = jnp.concatenate([marks, jnp.zeros((sent.shape[0] - 2 * tokens - MASKS, tokens), jnp.float32)], axis=0)
+    marks = jnp.concatenate([mask[...], jnp.zeros((sent.shape[0] - 2 * tokens - MASKS, tokens), jnp.float32)], axis=0)
     sent[2 * tokens :, :] = jnp.concatenate([marks] * (sent.shape[1] // tokens), axis=1).astype(jnp.bfloat16)
 
 
@@ -192,8 +205,10 @@
         summed[rows, :] = total
         mean = jnp.sum(total, axis=1, keepdims=True) / total.shape[1]
         off = total - mean
-        stats[0:1, rows] = column_to_row(mean)
-        stats[1:2, rows] = column_to_row(jnp.sum(off * off, axis=1, keepdims=True))
+        square = column_to_row(jnp.sum(off * off, axis=1, keepdims=True))
+        for copy in range(stats.shape[0]):
+            stats[copy, 2 * side : 2 * side + 1, :] = column_to_row(mean)
+            stats[copy, 2 * side + 1 : 2 * side + 2, :] = square
 
 
 def add_up(partial, arrived):
@@ -202,7 +217,7 @@
         add_kernel,
         out_shape=(
             jax.ShapeDtypeStruct((rows, width), jnp.float32),
-            jax.ShapeDtypeStruct((2, rows), jnp.float32),
+            jax.ShapeDtypeStruct((8, 4, rows // 2), jnp.float32),
         ),
         in_specs=[VMEM] * 2,
         out_specs=(VMEM, VMEM),
@@ -216,10 +231,10 @@
     errors = []
     for side, prediction in enumerate((pred, pred_far)):
         rows = slice(side * tokens, (side + 1) * tokens)
-        means = stats[:, 0, rows]
+        means = stats[:, 2 * side, :]
         mean = jnp.sum(means, axis=0, keepdims=True) * (width / D)
         shift = means - mean
-        var = jnp.sum(stats[:, 1, rows] + width * shift * shift, axis=0, keepdims=True) / D
+        var = jnp.sum(stats[:, 2 * side + 1, :] + width * shift * shift, axis=0, keepdims=True) / D
         scale = row_to_column(lax.rsqrt(var + 1e-06))
         value = ((summed[rows, :] - row_to_column(mean)) * scale).astype(jnp.bfloat16)
         if side == 0:
@@ -227,7 +242,7 @@
         value = value.astype(jnp.float32)
         for k in range(MASKS):
             if side == 0:
-                marks = mask[k : k + 1, :].astype(jnp.float32)
+                marks = mask[k : k + 1, :]
             else:
                 marks = arrived[rows_here + k : rows_here + k + 1, :tokens].astype(jnp.float32)
             difference = jnp.clip(prediction[k * tokens : (k + 1) * tokens, :] - value, -1.0, 1.0)
@@ -281,13 +296,9 @@
 
     hidden = pred_hidden.reshape(-1, pred_hidden.shape[2])
     hidden_far = neighbour(hidden)
-
-    def predict(states):
-        return jnp.dot(states, pred_weight, preferred_element_type=jnp.float32)
-
-    hidden_own, parts = lax.optimization_barrier((hidden, parts))
-    pred = predict(hidden_own)
-    weight, pred = lax.optimization_barrier((weight, pred))
+    mask, parts = lax.optimization_barrier((mask, parts))
+    marks = as_marks(mask)
+    weight, marks = lax.optimization_barrier((weight, marks))
     weights = [weight] + [lax.ppermute(weight, "x", ring(4, -d)) for d in (1, 2, 3)]
 
     parts = lax.all_to_all(parts, ("y", "z"), 0, 0, tiled=True)
@@ -297,10 +308,11 @@
     attended = lax.all_gather(attended, "w", axis=0)
     attended = lax.all_gather(attended, "c", axis=1).reshape((8,) + attended.shape[1:])
 
-    partial, sent = project(attended, residual, mask, weights)
+    partial, sent = project(attended, residual, marks, weights)
     arrived = neighbour(sent)
     hidden, hidden_far, sent = lax.optimization_barrier((hidden, hidden_far, sent))
-    pred_far = predict(hidden_far)
+    pred = jnp.dot(hidden, pred_weight, preferred_element_type=jnp.float32)
+    pred_far = jnp.dot(hidden_far, pred_weight, preferred_element_type=jnp.float32)
     z = lax.axis_index("z")
     hidden_rows = [
         lax.dynamic_index_in_dim(h.T.reshape(8, 4, 2, 16, -1), z, 2, keepdims=False)
@@ -310,8 +322,11 @@
     hidden_rows = hidden_rows.reshape(-1, 2 * hidden.shape[0])
 
     summed, stats = add_up(partial, arrived)
-    stats = lax.all_gather(stats, TENSOR, axis=0)
-    target, product = finish(stats, summed, arrived, mask, pred, pred_far, hidden_rows)
+    stats, pred, pred_far, hidden_rows = lax.optimization_barrier(
+        (stats, pred, pred_far, hidden_rows)
+    )
+    stats = lax.all_to_all(stats, TENSOR, 0, 0, tiled=True)
+    target, product = finish(stats, summed, arrived, marks, pred, pred_far, hidden_rows)
 
     product = lax.all_to_all(product.reshape(4, -1, width), "x", 0, 0, tiled=True)
     product = jnp.sum(product.astype(jnp.float32), axis=0).astype(jnp.bfloat16)

time: 159 us -> 156 us (0.981)
  blocking collectives: 67.3 us -> 64.9 us
    all_gather x1 -> x0, blocking collectives: 14.3 us -> none  [body(): stats = lax.all_gather(stats, TENSOR, axis=0)]
    all_to_all x0 -> x1, blocking collectives: none -> 12.1 us  [body(): stats = lax.all_to_all(stats, TENSOR, 0, 0, tiled=True)]
  transfers between devices with their start and end apart: 15 -> 15, of which waited for: 2 -> 2; matrix products, arithmetic and copies ran while one was open for 6% -> 5% of each run, Pallas kernels for 4% -> 5%
where the time goes in v4:
time: 156 us; the launch traced here: 155 us
  blocking collectives  64.9 us (42%)
  starting transfers between devices  56.9 us (36%)
  Pallas kernels  13.8 us (9%)
  waiting for transfers between devices  9.12 us (6%)
  local copies, waits for them, and re-layouts  4.76 us (3%)
  other arithmetic  2.44 us (2%)
  matrix products  2.26 us (1%)
    all_gather x1, blocking collectives, body(): attended = lax.all_gather(attended, 'w', axis=0)  19.4 us
    all_to_all x1, blocking collectives, body(): lax.all_to_all(product.reshape(8, -1, width), ('h', 'y'), 0, 0, tiled=True)  15.7 us
    all_to_all x1, blocking collectives, body(): lax.all_to_all(product.reshape(4, -1, width), 'x', 0, 0, tiled=True)  15.4 us
    ppermute x4, starting transfers between devices, neighbour(): return lax.ppermute(array, 'z', ring(2, 1))  15.1 us
    all_to_all x1, blocking collectives, body(): stats = lax.all_to_all(stats, TENSOR, 0, 0, tiled=True)  12.1 us
    ppermute x3, starting transfers between devices, body(): kvs = [kv_own] + [lax.ppermute(kv_own, 'x', ring(4, d)) for d in (2, 1, 3)]  11.1 us
    ppermute x4, waiting for transfers between devices, neighbour(): return lax.ppermute(array, 'z', ring(2, 1))  9.09 us
    ppermute x3, starting transfers between devices, body(): lax.ppermute(weight, 'x', ring(4, -d))  8.67 us
  transfers between devices with their start and end apart: 15, of which 2 were waited for; matrix products, arithmetic and copies ran while one was open for 5% of the time, Pallas kernels for 5%

profile of v4, /device:TPU:2, one launch (start us, length us, event | category | flops | bytes accessed | tf_op | source)
XLA Modules:
  0.0 155.2 jit_solution(7494066367431987334)
XLA Ops:
  0.6 0.0 copy-start
  0.7 0.6 pad_add_fusion.place
  1.2 2.1 %shard_map.95 = (bf16[3,128,128]{2,1,0:T(8,128)(2,1)}, bf16[3,128,128]{2,1,0:T(8,128)(2,1)}, bf16[3,128,128]{2,1,0:T(8,128)(2,1)}, bf16[3,128,128]{2,1,0:T(8,128)(2,1)}, bf16[8,48,768]{2,1,0:T(8,128)(2,1)}) custom-call(s32[3]{0:T(128)} %pad_add_fusion.place, bf16[128,384]{1,0:T(8,128)(2,1)} %queries.1, bf16[128,384]{1,0:T(8,128)(2,1)} %keys.1, ...), custom_call_target="tpu_custom_call" | custom-call | tf_op jit(solution)/shard_map/pallas_call | solution.py:61
  3.3 3.5 %collective-permute-start = (bf16[3,128,128]{2,1,0:T(8,128)(2,1)}, bf16[3,128,128]{2,1,0:T(8,128)(2,1)S(1)}, u32[]{:S(2)}, u32[]{:S(2)}) collective-permute-start(bf16[3,128,128]{2,1,0:T(8,128)(2,1)} %get-tuple-element.36), channel_id=1, source_target_pairs={{0,64},{64,0},{192,128},{1,65},{65,1},{193,129},{2,66},{66,2},{194... | collective-permute-start | bytes 294920 | tf_op jit(solution)/shard_map/ppermute | solution.py:284
  6.8 2.3 %collective-permute-start.1 = (bf16[3,128,128]{2,1,0:T(8,128)(2,1)}, bf16[3,128,128]{2,1,0:T(8,128)(2,1)S(1)}, u32[]{:S(2)}, u32[]{:S(2)}) collective-permute-start(bf16[3,128,128]{2,1,0:T(8,128)(2,1)} %get-tuple-element.39), channel_id=1, source_target_pairs={{0,128},{128,0},{192,64},{1,129},{129,1},{193,65},{2,130},{130,2},... | collective-permute-start | bytes 294920 | tf_op jit(solution)/shard_map/ppermute | solution.py:284
  9.1 1.3 collective-permute-start.2
  10.4 0.8 slice_bitcast_fusion.3
  11.3 0.0 collective-permute-done
  11.3 0.0 copy-start.2
  11.3 8.5 %all-to-all-start = ((bf16[8,48,768]{2,1,0:T(8,128)(2,1)}), bf16[8,48,768]{2,1,0:T(8,128)(2,1)S(1)}, u32[]{:S(2)}, u32[]{:S(2)}) async-start(bf16[8,48,768]{2,1,0:T(8,128)(2,1)} %get-tuple-element.41), calls=%async_computation | async-start | bytes 1179648 | tf_op jit(solution)/shard_map/all_to_all | solution.py:290
  19.7 0.0 collective-permute-done.1
  19.8 0.0 collective-permute-done.2
  19.8 3.8 %collective-permute-start.5 = (bf16[4,2,128,128]{3,2,1,0:T(8,128)(2,1)S(1)}, bf16[4,2,128,128]{3,2,1,0:T(8,128)(2,1)S(1)}, u32[]{:S(2)}, u32[]{:S(2)}) collective-permute-start(bf16[4,2,128,128]{3,2,1,0:T(8,128)(2,1)S(1)} %pad_maximum_fusion.kv0), channel_id=1, source_target_pairs={{0,48},{16,0},{32,16},{48,32},{1,49},{17,1},{33,17},{49,33},{2,50}... | collective-permute-start | bytes 786440 | tf_op jit(solution)/shard_map/ppermute | solution.py:292
  23.6 2.1 %collective-permute-start.4 = (bf16[4,2,128,128]{3,2,1,0:T(8,128)(2,1)S(1)}, bf16[4,2,128,128]{3,2,1,0:T(8,128)(2,1)S(1)}, u32[]{:S(2)}, u32[]{:S(2)}) collective-permute-start(bf16[4,2,128,128]{3,2,1,0:T(8,128)(2,1)S(1)} %pad_maximum_fusion.kv0), channel_id=1, source_target_pairs={{0,16},{16,32},{32,48},{48,0},{1,17},{17,33},{33,49},{49,1},{2,18}... | collective-permute-start | bytes 786440 | tf_op jit(solution)/shard_map/ppermute | solution.py:292
  25.7 5.2 %collective-permute-start.3 = (bf16[4,2,128,128]{3,2,1,0:T(8,128)(2,1)S(1)}, bf16[4,2,128,128]{3,2,1,0:T(8,128)(2,1)S(1)}, u32[]{:S(2)}, u32[]{:S(2)}) collective-permute-start(bf16[4,2,128,128]{3,2,1,0:T(8,128)(2,1)S(1)} %pad_maximum_fusion.kv0), channel_id=1, source_target_pairs={{0,32},{16,48},{32,0},{48,16},{1,33},{17,49},{33,1},{49,17},{2,34}... | collective-permute-start | bytes 786440 | tf_op jit(solution)/shard_map/ppermute | solution.py:292
  30.9 0.8 slice.24
  31.8 4.3 %collective-permute-start.6 = (bf16[4,128,128]{2,1,0:T(8,128)(2,1)S(1)}, bf16[4,128,128]{2,1,0:T(8,128)(2,1)S(1)}, u32[]{:S(2)}, u32[]{:S(2)}) collective-permute-start(bf16[4,128,128]{2,1,0:T(8,128)(2,1)S(1)} %pad_maximum_fusion.1.q_own), channel_id=1, source_target_pairs={{0,8},{8,0},{1,9},{9,1},{2,10},{10,2},{3,11},{11,3},{4,12},{12,4},... | collective-permute-start | bytes 393224 | tf_op jit(solution)/shard_map/ppermute | solution.py:32
  36.1 2.1 %copy.17 = bf16[256,1024]{0,1:T(8,128)(2,1)} copy(bf16[256,1024]{1,0:T(8,128)(2,1)} %bitcast.39) | data formatting | bytes 1048576 | tf_op jit(solution)/shard_map/reshape | solution.py:297
  38.1 1.9 %collective-permute-start.7 = (bf16[256,1024]{0,1:T(8,128)(2,1)}, bf16[256,1024]{0,1:T(8,128)(2,1)}, u32[]{:S(2)}, u32[]{:S(2)}) collective-permute-start(bf16[256,1024]{0,1:T(8,128)(2,1)} %copy.17), channel_id=1, source_target_pairs={{0,8},{8,0},{1,9},{9,1},{2,10},{10,2},{3,11},{11,3},{4,12},{12,4},... | collective-permute-start | bytes 1572872 | tf_op jit(solution)/shard_map/ppermute | solution.py:32
  40.0 0.0 collective-permute-done.6.q_far
  40.0 0.0 collective-permute-done.5.kv3
  40.0 0.0 collective-permute-done.4.kv2
  40.1 0.0 collective-permute-done.3.kv1
  40.1 0.0 all-to-all-done.one
  40.1 0.0 copy-done.2
  40.1 4.7 %shard_map.96 = bf16[8,144,128]{2,1,0:T(8,128)(2,1)} custom-call(s32[3]{0:T(128)S(1)} %copy-done.2, bf16[4,128,128]{2,1,0:T(8,128)(2,1)S(1)} %pad_maximum_fusion.1.q_own, bf16[4,128,128]{2,1,0:T(8,128)(2,1)S(1)} %collective-permute-done.6.q_far, bf16[4,2,128,128]{3,2,1,0:T(8,128)(2,1)S(1)} %pad_maximum_fusion.kv0, ...), custom_call_target="tpu_custom_call" | custom-call | flops 1073741824 | bytes 2097152 | tf_op jit(solution)/shard_map/pallas_call | solution.py:103
  44.8 6.5 %all-to-all-start.1 = ((bf16[8,144,128]{2,1,0:T(8,128)(2,1)}), bf16[8,144,128]{2,1,0:T(8,128)(2,1)}, u32[]{:S(2)}, u32[]{:S(2)}) async-start(bf16[8,144,128]{2,1,0:T(8,128)(2,1)} %shard_map.96), calls=%async_computation.1 | async-start | bytes 589824 | tf_op jit(solution)/shard_map/all_to_all | solution.py:304
  51.3 1.2 shard_map.98.mask
  52.6 0.0 copy-start.1
  52.6 0.0 copy-start.3
  52.6 2.0 %collective-permute-start.11 = (bf16[8,48,768]{2,1,0:T(8,128)(2,1)S(1)}, bf16[8,48,768]{2,1,0:T(8,128)(2,1)S(1)}, u32[]{:S(2)}, u32[]{:S(2)}) collective-permute-start(bf16[8,48,768]{2,1,0:T(8,128)(2,1)S(1)} %all-to-all-done.one), channel_id=1, source_target_pairs={{0,16},{16,32},{32,48},{48,0},{1,17},{17,33},{33,49},{49,1},{2,18}... | collective-permute-start | bytes 1769480 | tf_op jit(solution)/shard_map/ppermute | solution.py:302
  54.6 4.4 %collective-permute-start.10 = (bf16[8,48,768]{2,1,0:T(8,128)(2,1)S(1)}, bf16[8,48,768]{2,1,0:T(8,128)(2,1)S(1)}, u32[]{:S(2)}, u32[]{:S(2)}) collective-permute-start(bf16[8,48,768]{2,1,0:T(8,128)(2,1)S(1)} %all-to-all-done.one), channel_id=1, source_target_pairs={{0,32},{16,48},{32,0},{48,16},{1,33},{17,49},{33,1},{49,17},{2,34}... | collective-permute-start | bytes 1769480 | tf_op jit(solution)/shard_map/ppermute | solution.py:302
  59.0 2.2 %collective-permute-start.9 = (bf16[8,48,768]{2,1,0:T(8,128)(2,1)S(1)}, bf16[8,48,768]{2,1,0:T(8,128)(2,1)}, u32[]{:S(2)}, u32[]{:S(2)}) collective-permute-start(bf16[8,48,768]{2,1,0:T(8,128)(2,1)S(1)} %all-to-all-done.one), channel_id=1, source_target_pairs={{0,48},{16,0},{32,16},{48,32},{1,49},{17,1},{33,17},{49,33},{2,50}... | collective-permute-start | bytes 1769480 | tf_op jit(solution)/shard_map/ppermute | solution.py:302
  61.3 0.0 collective-permute-done.7
  61.3 0.0 all-to-all-done.1.chunks
  61.3 2.0 %shard_map.97 = (bf16[128,192]{1,0:T(8,128)(2,1)}, bf16[128,192]{1,0:T(8,128)(2,1)}) custom-call(s32[3]{0:T(128)} %pad_add_fusion.place, bf16[8,144,128]{2,1,0:T(8,128)(2,1)} %all-to-all-done.1.chunks), custom_call_target="tpu_custom_call" | custom-call | tf_op jit(solution)/shard_map/pallas_call | solution.py:144
  63.3 3.9 %collective-permute-start.8 = (bf16[128,192]{1,0:T(8,128)(2,1)}, bf16[128,192]{1,0:T(8,128)(2,1)}, u32[]{:S(2)}, u32[]{:S(2)}) collective-permute-start(bf16[128,192]{1,0:T(8,128)(2,1)} %get-tuple-element.50), channel_id=1, source_target_pairs={{0,8},{8,0},{1,9},{9,1},{2,10},{10,2},{3,11},{11,3},{4,12},{12,4},... | collective-permute-start | bytes 147464 | tf_op jit(solution)/shard_map/ppermute | solution.py:32
  67.3 2.5 %collective-permute-done.8 = bf16[128,192]{1,0:T(8,128)(2,1)} collective-permute-done((bf16[128,192]{1,0:T(8,128)(2,1)}, bf16[128,192]{1,0:T(8,128)(2,1)}, u32[]{:S(2)}, u32[]{:S(2)}) %collective-permute-start.8) | collective-permute-done | bytes 49184 | tf_op jit(solution)/shard_map/ppermute | solution.py:32
  69.8 1.0 pad_maximum_fusion.2
  70.8 19.4 %all-gather = bf16[512,384]{1,0:T(8,128)(2,1)S(1)} all-gather(bf16[128,384]{1,0:T(8,128)(2,1)S(1)} %pad_maximum_fusion.2), channel_id=2, replica_groups=mesh['h'=2,'y'=4,'x'=4,'z'=2,'w'=4,'c'=2] {'w'}, dimensions={0}, use_global_device_ids=true | all-gather | bytes 491520 | tf_op jit(solution)/shard_map/all_gather | solution.py:308
  90.1 2.4 %all-gather.1 = bf16[4,256,384]{2,1,0:T(8,128)(2,1)S(1)} all-gather(bf16[4,128,384]{2,1,0:T(8,128)(2,1)S(1)} %bitcast.37), channel_id=3, replica_groups=mesh['h'=2,'y'=4,'x'=4,'z'=2,'w'=4,'c'=2] {'c'}, dimensions={1}, use_global_device_ids=true | all-gather | bytes 1179648 | tf_op jit(solution)/shard_map/all_gather | solution.py:309
  92.5 0.0 collective-permute-done.11.four
  92.5 0.0 collective-permute-done.10.three
  92.5 0.0 collective-permute-done.9.two
  92.5 0.0 copy-done.1
  92.5 0.0 copy-done.3
  92.5 0.0 copy-start.4
  92.5 2.1 %shard_map.99 = (f32[256,768]{1,0:T(8,128)S(1)}, bf16[272,768]{1,0:T(8,128)(2,1)S(1)}) custom-call(bf16[8,128,384]{2,1,0:T(8,128)(2,1)S(1)} %bitcast.33, bf16[128,768]{1,0:T(8,128)(2,1)S(1)} %copy-done.1, f32[2,128]{1,0:T(2,128)S(1)} %copy-done.3, bf16[8,48,768]{2,1,0:T(8,128)(2,1)S(1)} %all-to-all-done.one, bf16[8,48,768]{2,1,0:T(8,128)(2,1)} %collective-permute-done.9.two, ...), custom_call_target="tpu_custom_call" | custom-call | flops 603979776 | bytes 2359296 | tf_op jit(solution)/shard_map/pallas_call | solution.py:184
  94.7 5.0 %collective-permute-start.12 = (bf16[272,768]{1,0:T(8,128)(2,1)S(1)}, bf16[272,768]{1,0:T(8,128)(2,1)S(1)}, u32[]{:S(2)}, u32[]{:S(2)}) collective-permute-start(bf16[272,768]{1,0:T(8,128)(2,1)S(1)} %get-tuple-element.56), channel_id=1, source_target_pairs={{0,8},{8,0},{1,9},{9,1},{2,10},{10,2},{3,11},{11,3},{4,12},{12,4},... | collective-permute-start | bytes 1253384 | tf_op jit(solution)/shard_map/ppermute | solution.py:32
  99.6 0.0 copy-done
  99.6 0.0 copy-done.4
  99.6 0.6 fusion.pred
  100.3 1.0 dynamic-slice_bitcast_fusion
  101.3 0.1 maximum_bitcast_fusion
  101.4 1.6 %fusion.1.pred_far = f32[256,768]{1,0:T(8,128)S(1)} fusion(bf16[256,1024]{0,1:T(8,128)(2,1)} %collective-permute-done.7, bf16[1024,768]{1,0:T(8,128)(2,1)S(1)} %copy-done), kind=kOutput, calls=%fused_computation.14 | convolution fusion | flops 402653184 | bytes 2883584 | tf_op jit(solution)/shard_map/dot_general | solution.py:315
  103.0 6.5 %collective-permute-done.12.arrived = bf16[272,768]{1,0:T(8,128)(2,1)S(1)} collective-permute-done((bf16[272,768]{1,0:T(8,128)(2,1)S(1)}, bf16[272,768]{1,0:T(8,128)(2,1)S(1)}, u32[]{:S(2)}, u32[]{:S(2)}) %collective-permute-start.12) | collective-permute-done | bytes 417824 | tf_op jit(solution)/shard_map/ppermute | solution.py:32
  109.6 0.3 shard_map.100
  109.8 12.1 %all_to_all.25.stats = f32[8,4,128]{2,1,0:T(4,128)S(1)} all-to-all(f32[8,4,128]{2,1,0:T(4,128)S(1)} %get-tuple-element.61), channel_id=1, replica_groups=mesh['h'=2,'y'=4,'x'=4,'z'=2,'w'=4,'c'=2] {'w','c'}, dimensions={0} | all-to-all | bytes 32768 | tf_op jit(solution)/shard_map/all_to_all | solution.py:328
  121.9 1.4 shard_map.101
  123.3 15.4 %all_to_all.26 = bf16[4,128,768]{2,1,0:T(8,128)(2,1)S(1)} all-to-all(bf16[4,128,768]{2,1,0:T(8,128)(2,1)S(1)} %bitcast.35), channel_id=1, replica_groups=mesh['h'=2,'y'=4,'x'=4,'z'=2,'w'=4,'c'=2] {'x'}, dimensions={0} | all-to-all | bytes 1572864 | tf_op jit(solution)/shard_map/all_to_all | solution.py:331
  138.7 0.1 reduce_sum.21
  138.8 15.7 %all_to_all.27 = bf16[8,16,768]{2,1,0:T(8,128)(2,1)S(1)} all-to-all(bf16[8,16,768]{2,1,0:T(8,128)(2,1)S(1)} %bitcast.38), channel_id=1, replica_groups=mesh['h'=2,'y'=4,'x'=4,'z'=2,'w'=4,'c'=2] {'h','y'}, dimensions={0} | all-to-all | bytes 393216 | tf_op jit(solution)/shard_map/all_to_all | solution.py:333
  154.5 0.6 broadcast_multiply_fusion
  (10 shorter events, 0.2 us)
Async XLA Ops:
  0.6 99.0 %copy-start = (bf16[1024,768]{1,0:T(8,128)(2,1)S(1)}, bf16[1024,768]{1,0:T(8,128)(2,1)}, u32[]{:S(2)}) copy-start(bf16[1024,768]{1,0:T(8,128)(2,1)} %param.14) | copy-start | bytes 4718596
  3.3 7.9 %collective-permute-start = (bf16[3,128,128]{2,1,0:T(8,128)(2,1)}, bf16[3,128,128]{2,1,0:T(8,128)(2,1)S(1)}, u32[]{:S(2)}, u32[]{:S(2)}) collective-permute-start(bf16[3,128,128]{2,1,0:T(8,128)(2,1)} %get-tuple-element.36), channel_id=1, source_target_pairs={{0,64},{64,0},{192,128},{1,65},{65,1},{193,129},{2,66},{66,2},{194... | collective-permute-start | bytes 294920 | tf_op jit(solution)/shard_map/ppermute | solution.py:284
  6.8 12.9 %collective-permute-start.1 = (bf16[3,128,128]{2,1,0:T(8,128)(2,1)}, bf16[3,128,128]{2,1,0:T(8,128)(2,1)S(1)}, u32[]{:S(2)}, u32[]{:S(2)}) collective-permute-start(bf16[3,128,128]{2,1,0:T(8,128)(2,1)} %get-tuple-element.39), channel_id=1, source_target_pairs={{0,128},{128,0},{192,64},{1,129},{129,1},{193,65},{2,130},{130,2},... | collective-permute-start | bytes 294920 | tf_op jit(solution)/shard_map/ppermute | solution.py:284
  9.1 10.7 %collective-permute-start.2 = (bf16[3,128,128]{2,1,0:T(8,128)(2,1)}, bf16[3,128,128]{2,1,0:T(8,128)(2,1)S(1)}, u32[]{:S(2)}, u32[]{:S(2)}) collective-permute-start(bf16[3,128,128]{2,1,0:T(8,128)(2,1)} %get-tuple-element.40), channel_id=1, source_target_pairs={{64,128},{128,64},{192,0},{65,129},{129,65},{193,1},{66,130},{130,... | collective-permute-start | bytes 294920 | tf_op jit(solution)/shard_map/ppermute | solution.py:284
  11.3 28.8 %copy-start.2 = (s32[3]{0:T(128)S(1)}, s32[3]{0:T(128)}, u32[]{:S(2)}) copy-start(s32[3]{0:T(128)} %pad_add_fusion.place) | copy-start | bytes 40
  11.3 28.8 %all-to-all-start = ((bf16[8,48,768]{2,1,0:T(8,128)(2,1)}), bf16[8,48,768]{2,1,0:T(8,128)(2,1)S(1)}, u32[]{:S(2)}, u32[]{:S(2)}) async-start(bf16[8,48,768]{2,1,0:T(8,128)(2,1)} %get-tuple-element.41), calls=%async_computation | async-start | bytes 1179648 | tf_op jit(solution)/shard_map/all_to_all | solution.py:290
  19.8 20.2 %collective-permute-start.5 = (bf16[4,2,128,128]{3,2,1,0:T(8,128)(2,1)S(1)}, bf16[4,2,128,128]{3,2,1,0:T(8,128)(2,1)S(1)}, u32[]{:S(2)}, u32[]{:S(2)}) collective-permute-start(bf16[4,2,128,128]{3,2,1,0:T(8,128)(2,1)S(1)} %pad_maximum_fusion.kv0), channel_id=1, source_target_pairs={{0,48},{16,0},{32,16},{48,32},{1,49},{17,1},{33,17},{49,33},{2,50}... | collective-permute-start | bytes 786440 | tf_op jit(solution)/shard_map/ppermute | solution.py:292
  23.6 16.4 %collective-permute-start.4 = (bf16[4,2,128,128]{3,2,1,0:T(8,128)(2,1)S(1)}, bf16[4,2,128,128]{3,2,1,0:T(8,128)(2,1)S(1)}, u32[]{:S(2)}, u32[]{:S(2)}) collective-permute-start(bf16[4,2,128,128]{3,2,1,0:T(8,128)(2,1)S(1)} %pad_maximum_fusion.kv0), channel_id=1, source_target_pairs={{0,16},{16,32},{32,48},{48,0},{1,17},{17,33},{33,49},{49,1},{2,18}... | collective-permute-start | bytes 786440 | tf_op jit(solution)/shard_map/ppermute | solution.py:292
  25.7 14.4 %collective-permute-start.3 = (bf16[4,2,128,128]{3,2,1,0:T(8,128)(2,1)S(1)}, bf16[4,2,128,128]{3,2,1,0:T(8,128)(2,1)S(1)}, u32[]{:S(2)}, u32[]{:S(2)}) collective-permute-start(bf16[4,2,128,128]{3,2,1,0:T(8,128)(2,1)S(1)} %pad_maximum_fusion.kv0), channel_id=1, source_target_pairs={{0,32},{16,48},{32,0},{48,16},{1,33},{17,49},{33,1},{49,17},{2,34}... | collective-permute-start | bytes 786440 | tf_op jit(solution)/shard_map/ppermute | solution.py:292
  31.8 8.3 %collective-permute-start.6 = (bf16[4,128,128]{2,1,0:T(8,128)(2,1)S(1)}, bf16[4,128,128]{2,1,0:T(8,128)(2,1)S(1)}, u32[]{:S(2)}, u32[]{:S(2)}) collective-permute-start(bf16[4,128,128]{2,1,0:T(8,128)(2,1)S(1)} %pad_maximum_fusion.1.q_own), channel_id=1, source_target_pairs={{0,8},{8,0},{1,9},{9,1},{2,10},{10,2},{3,11},{11,3},{4,12},{12,4},... | collective-permute-start | bytes 393224 | tf_op jit(solution)/shard_map/ppermute | solution.py:32
  38.1 23.2 %collective-permute-start.7 = (bf16[256,1024]{0,1:T(8,128)(2,1)}, bf16[256,1024]{0,1:T(8,128)(2,1)}, u32[]{:S(2)}, u32[]{:S(2)}) collective-permute-start(bf16[256,1024]{0,1:T(8,128)(2,1)} %copy.17), channel_id=1, source_target_pairs={{0,8},{8,0},{1,9},{9,1},{2,10},{10,2},{3,11},{11,3},{4,12},{12,4},... | collective-permute-start | bytes 1572872 | tf_op jit(solution)/shard_map/ppermute | solution.py:32
  44.8 16.5 %all-to-all-start.1 = ((bf16[8,144,128]{2,1,0:T(8,128)(2,1)}), bf16[8,144,128]{2,1,0:T(8,128)(2,1)}, u32[]{:S(2)}, u32[]{:S(2)}) async-start(bf16[8,144,128]{2,1,0:T(8,128)(2,1)} %shard_map.96), calls=%async_computation.1 | async-start | bytes 589824 | tf_op jit(solution)/shard_map/all_to_all | solution.py:304
  52.6 39.9 %copy-start.1 = (bf16[128,768]{1,0:T(8,128)(2,1)S(1)}, bf16[128,768]{1,0:T(8,128)(2,1)}, u32[]{:S(2)}) copy-start(bf16[128,768]{1,0:T(8,128)(2,1)} %residual.1) | copy-start | bytes 589828
  52.6 39.9 %copy-start.3 = (f32[2,128]{1,0:T(2,128)S(1)}, f32[2,128]{1,0:T(2,128)}, u32[]{:S(2)}) copy-start(f32[2,128]{1,0:T(2,128)} %shard_map.98.mask) | copy-start | bytes 3076
  52.6 39.9 %collective-permute-start.11 = (bf16[8,48,768]{2,1,0:T(8,128)(2,1)S(1)}, bf16[8,48,768]{2,1,0:T(8,128)(2,1)S(1)}, u32[]{:S(2)}, u32[]{:S(2)}) collective-permute-start(bf16[8,48,768]{2,1,0:T(8,128)(2,1)S(1)} %all-to-all-done.one), channel_id=1, source_target_pairs={{0,16},{16,32},{32,48},{48,0},{1,17},{17,33},{33,49},{49,1},{2,18}... | collective-permute-start | bytes 1769480 | tf_op jit(solution)/shard_map/ppermute | solution.py:302
  54.6 37.9 %collective-permute-start.10 = (bf16[8,48,768]{2,1,0:T(8,128)(2,1)S(1)}, bf16[8,48,768]{2,1,0:T(8,128)(2,1)S(1)}, u32[]{:S(2)}, u32[]{:S(2)}) collective-permute-start(bf16[8,48,768]{2,1,0:T(8,128)(2,1)S(1)} %all-to-all-done.one), channel_id=1, source_target_pairs={{0,32},{16,48},{32,0},{48,16},{1,33},{17,49},{33,1},{49,17},{2,34}... | collective-permute-start | bytes 1769480 | tf_op jit(solution)/shard_map/ppermute | solution.py:302
  59.0 33.5 %collective-permute-start.9 = (bf16[8,48,768]{2,1,0:T(8,128)(2,1)S(1)}, bf16[8,48,768]{2,1,0:T(8,128)(2,1)}, u32[]{:S(2)}, u32[]{:S(2)}) collective-permute-start(bf16[8,48,768]{2,1,0:T(8,128)(2,1)S(1)} %all-to-all-done.one), channel_id=1, source_target_pairs={{0,48},{16,0},{32,16},{48,32},{1,49},{17,1},{33,17},{49,33},{2,50}... | collective-permute-start | bytes 1769480 | tf_op jit(solution)/shard_map/ppermute | solution.py:302
  63.3 6.5 %collective-permute-start.8 = (bf16[128,192]{1,0:T(8,128)(2,1)}, bf16[128,192]{1,0:T(8,128)(2,1)}, u32[]{:S(2)}, u32[]{:S(2)}) collective-permute-start(bf16[128,192]{1,0:T(8,128)(2,1)} %get-tuple-element.50), channel_id=1, source_target_pairs={{0,8},{8,0},{1,9},{9,1},{2,10},{10,2},{3,11},{11,3},{4,12},{12,4},... | collective-permute-start | bytes 147464 | tf_op jit(solution)/shard_map/ppermute | solution.py:32
  92.5 7.1 %copy-start.4 = (bf16[256,1024]{0,1:T(8,128)(2,1)S(1)}, bf16[256,1024]{0,1:T(8,128)(2,1)}, u32[]{:S(2)}) copy-start(bf16[256,1024]{0,1:T(8,128)(2,1)} %copy.17) | copy-start | bytes 1572868
  94.7 14.9 %collective-permute-start.12 = (bf16[272,768]{1,0:T(8,128)(2,1)S(1)}, bf16[272,768]{1,0:T(8,128)(2,1)S(1)}, u32[]{:S(2)}, u32[]{:S(2)}) collective-permute-start(bf16[272,768]{1,0:T(8,128)(2,1)S(1)} %get-tuple-element.56), channel_id=1, source_target_pairs={{0,8},{8,0},{1,9},{9,1},{2,10},{10,2},{3,11},{11,3},{4,12},{12,4},... | collective-permute-start | bytes 1253384 | tf_op jit(solution)/shard_map/ppermute | solution.py:32

commit v5 on v4

--- a/solution.py
+++ b/solution.py
@@ -244,7 +244,7 @@
             if side == 0:
                 marks = mask[k : k + 1, :]
             else:
-                marks = arrived[rows_here + k : rows_here + k + 1, :tokens].astype(jnp.float32)
+                marks = arrived[rows_here:, :tokens].astype(jnp.float32)[k : k + 1]
             difference = jnp.clip(prediction[k * tokens : (k + 1) * tokens, :] - value, -1.0, 1.0)
             errors.append((difference * row_to_column(marks)).astype(jnp.bfloat16))
     error = jnp.concatenate(errors, axis=0)

time: 156 us -> 156 us (level)
  no operation moved by 1% of the time
where the time goes in v5:
time: 156 us; the launch traced here: 155 us
  blocking collectives  64.9 us (42%)
  starting transfers between devices  56.9 us (36%)
  Pallas kernels  13.8 us (9%)
  waiting for transfers between devices  9.12 us (6%)
  local copies, waits for them, and re-layouts  4.76 us (3%)
  other arithmetic  2.44 us (2%)
  matrix products  2.26 us (1%)
    all_gather x1, blocking collectives, body(): attended = lax.all_gather(attended, 'w', axis=0)  19.4 us
    all_to_all x1, blocking collectives, body(): lax.all_to_all(product.reshape(8, -1, width), ('h', 'y'), 0, 0, tiled=True)  15.7 us
    all_to_all x1, blocking collectives, body(): lax.all_to_all(product.reshape(4, -1, width), 'x', 0, 0, tiled=True)  15.4 us
    ppermute x4, starting transfers between devices, neighbour(): return lax.ppermute(array, 'z', ring(2, 1))  15.1 us
    all_to_all x1, blocking collectives, body(): stats = lax.all_to_all(stats, TENSOR, 0, 0, tiled=True)  12.1 us
    ppermute x3, starting transfers between devices, body(): kvs = [kv_own] + [lax.ppermute(kv_own, 'x', ring(4, d)) for d in (2, 1, 3)]  11.1 us
    ppermute x4, waiting for transfers between devices, neighbour(): return lax.ppermute(array, 'z', ring(2, 1))  9.09 us
    ppermute x3, starting transfers between devices, body(): lax.ppermute(weight, 'x', ring(4, -d))  8.67 us
  transfers between devices with their start and end apart: 15, of which 2 were waited for; matrix products, arithmetic and copies ran while one was open for 5% of the time, Pallas kernels for 5%

profile of v5, /device:TPU:2, one launch (start us, length us, event | category | flops | bytes accessed | tf_op | source)
XLA Modules:
  0.0 155.2 jit_solution(16163781310498858859)
XLA Ops:
  0.6 0.0 copy-start
  0.7 0.6 pad_add_fusion.place
  1.2 2.1 %shard_map.95 = (bf16[3,128,128]{2,1,0:T(8,128)(2,1)}, bf16[3,128,128]{2,1,0:T(8,128)(2,1)}, bf16[3,128,128]{2,1,0:T(8,128)(2,1)}, bf16[3,128,128]{2,1,0:T(8,128)(2,1)}, bf16[8,48,768]{2,1,0:T(8,128)(2,1)}) custom-call(s32[3]{0:T(128)} %pad_add_fusion.place, bf16[128,384]{1,0:T(8,128)(2,1)} %queries.1, bf16[128,384]{1,0:T(8,128)(2,1)} %keys.1, ...), custom_call_target="tpu_custom_call" | custom-call | tf_op jit(solution)/shard_map/pallas_call | solution.py:61
  3.3 3.5 %collective-permute-start = (bf16[3,128,128]{2,1,0:T(8,128)(2,1)}, bf16[3,128,128]{2,1,0:T(8,128)(2,1)S(1)}, u32[]{:S(2)}, u32[]{:S(2)}) collective-permute-start(bf16[3,128,128]{2,1,0:T(8,128)(2,1)} %get-tuple-element.36), channel_id=1, source_target_pairs={{0,64},{64,0},{192,128},{1,65},{65,1},{193,129},{2,66},{66,2},{194... | collective-permute-start | bytes 294920 | tf_op jit(solution)/shard_map/ppermute | solution.py:284
  6.8 2.3 %collective-permute-start.1 = (bf16[3,128,128]{2,1,0:T(8,128)(2,1)}, bf16[3,128,128]{2,1,0:T(8,128)(2,1)S(1)}, u32[]{:S(2)}, u32[]{:S(2)}) collective-permute-start(bf16[3,128,128]{2,1,0:T(8,128)(2,1)} %get-tuple-element.39), channel_id=1, source_target_pairs={{0,128},{128,0},{192,64},{1,129},{129,1},{193,65},{2,130},{130,2},... | collective-permute-start | bytes 294920 | tf_op jit(solution)/shard_map/ppermute | solution.py:284
  9.1 1.3 collective-permute-start.2
  10.4 0.8 slice_bitcast_fusion.3
  11.3 0.0 collective-permute-done
  11.3 0.0 copy-start.2
  11.3 8.5 %all-to-all-start = ((bf16[8,48,768]{2,1,0:T(8,128)(2,1)}), bf16[8,48,768]{2,1,0:T(8,128)(2,1)S(1)}, u32[]{:S(2)}, u32[]{:S(2)}) async-start(bf16[8,48,768]{2,1,0:T(8,128)(2,1)} %get-tuple-element.41), calls=%async_computation | async-start | bytes 1179648 | tf_op jit(solution)/shard_map/all_to_all | solution.py:290
  19.7 0.0 collective-permute-done.1
  19.8 0.0 collective-permute-done.2
  19.8 3.8 %collective-permute-start.5 = (bf16[4,2,128,128]{3,2,1,0:T(8,128)(2,1)S(1)}, bf16[4,2,128,128]{3,2,1,0:T(8,128)(2,1)S(1)}, u32[]{:S(2)}, u32[]{:S(2)}) collective-permute-start(bf16[4,2,128,128]{3,2,1,0:T(8,128)(2,1)S(1)} %pad_maximum_fusion.kv0), channel_id=1, source_target_pairs={{0,48},{16,0},{32,16},{48,32},{1,49},{17,1},{33,17},{49,33},{2,50}... | collective-permute-start | bytes 786440 | tf_op jit(solution)/shard_map/ppermute | solution.py:292
  23.6 2.1 %collective-permute-start.4 = (bf16[4,2,128,128]{3,2,1,0:T(8,128)(2,1)S(1)}, bf16[4,2,128,128]{3,2,1,0:T(8,128)(2,1)S(1)}, u32[]{:S(2)}, u32[]{:S(2)}) collective-permute-start(bf16[4,2,128,128]{3,2,1,0:T(8,128)(2,1)S(1)} %pad_maximum_fusion.kv0), channel_id=1, source_target_pairs={{0,16},{16,32},{32,48},{48,0},{1,17},{17,33},{33,49},{49,1},{2,18}... | collective-permute-start | bytes 786440 | tf_op jit(solution)/shard_map/ppermute | solution.py:292
  25.7 5.2 %collective-permute-start.3 = (bf16[4,2,128,128]{3,2,1,0:T(8,128)(2,1)S(1)}, bf16[4,2,128,128]{3,2,1,0:T(8,128)(2,1)S(1)}, u32[]{:S(2)}, u32[]{:S(2)}) collective-permute-start(bf16[4,2,128,128]{3,2,1,0:T(8,128)(2,1)S(1)} %pad_maximum_fusion.kv0), channel_id=1, source_target_pairs={{0,32},{16,48},{32,0},{48,16},{1,33},{17,49},{33,1},{49,17},{2,34}... | collective-permute-start | bytes 786440 | tf_op jit(solution)/shard_map/ppermute | solution.py:292
  30.9 0.8 slice.24
  31.8 4.3 %collective-permute-start.6 = (bf16[4,128,128]{2,1,0:T(8,128)(2,1)S(1)}, bf16[4,128,128]{2,1,0:T(8,128)(2,1)S(1)}, u32[]{:S(2)}, u32[]{:S(2)}) collective-permute-start(bf16[4,128,128]{2,1,0:T(8,128)(2,1)S(1)} %pad_maximum_fusion.1.q_own), channel_id=1, source_target_pairs={{0,8},{8,0},{1,9},{9,1},{2,10},{10,2},{3,11},{11,3},{4,12},{12,4},... | collective-permute-start | bytes 393224 | tf_op jit(solution)/shard_map/ppermute | solution.py:32
  36.1 2.1 %copy.17 = bf16[256,1024]{0,1:T(8,128)(2,1)} copy(bf16[256,1024]{1,0:T(8,128)(2,1)} %bitcast.39) | data formatting | bytes 1048576 | tf_op jit(solution)/shard_map/reshape | solution.py:297
  38.1 1.9 %collective-permute-start.7 = (bf16[256,1024]{0,1:T(8,128)(2,1)}, bf16[256,1024]{0,1:T(8,128)(2,1)}, u32[]{:S(2)}, u32[]{:S(2)}) collective-permute-start(bf16[256,1024]{0,1:T(8,128)(2,1)} %copy.17), channel_id=1, source_target_pairs={{0,8},{8,0},{1,9},{9,1},{2,10},{10,2},{3,11},{11,3},{4,12},{12,4},... | collective-permute-start | bytes 1572872 | tf_op jit(solution)/shard_map/ppermute | solution.py:32
  40.0 0.0 collective-permute-done.6.q_far
  40.0 0.0 collective-permute-done.5.kv3
  40.0 0.0 collective-permute-done.4.kv2
  40.1 0.0 collective-permute-done.3.kv1
  40.1 0.0 all-to-all-done.one
  40.1 0.0 copy-done.2
  40.1 4.7 %shard_map.96 = bf16[8,144,128]{2,1,0:T(8,128)(2,1)} custom-call(s32[3]{0:T(128)S(1)} %copy-done.2, bf16[4,128,128]{2,1,0:T(8,128)(2,1)S(1)} %pad_maximum_fusion.1.q_own, bf16[4,128,128]{2,1,0:T(8,128)(2,1)S(1)} %collective-permute-done.6.q_far, bf16[4,2,128,128]{3,2,1,0:T(8,128)(2,1)S(1)} %pad_maximum_fusion.kv0, ...), custom_call_target="tpu_custom_call" | custom-call | flops 1073741824 | bytes 2097152 | tf_op jit(solution)/shard_map/pallas_call | solution.py:103
  44.8 6.5 %all-to-all-start.1 = ((bf16[8,144,128]{2,1,0:T(8,128)(2,1)}), bf16[8,144,128]{2,1,0:T(8,128)(2,1)}, u32[]{:S(2)}, u32[]{:S(2)}) async-start(bf16[8,144,128]{2,1,0:T(8,128)(2,1)} %shard_map.96), calls=%async_computation.1 | async-start | bytes 589824 | tf_op jit(solution)/shard_map/all_to_all | solution.py:304
  51.3 1.2 shard_map.98.mask
  52.6 0.0 copy-start.1
  52.6 0.0 copy-start.3
  52.6 2.0 %collective-permute-start.11 = (bf16[8,48,768]{2,1,0:T(8,128)(2,1)S(1)}, bf16[8,48,768]{2,1,0:T(8,128)(2,1)S(1)}, u32[]{:S(2)}, u32[]{:S(2)}) collective-permute-start(bf16[8,48,768]{2,1,0:T(8,128)(2,1)S(1)} %all-to-all-done.one), channel_id=1, source_target_pairs={{0,16},{16,32},{32,48},{48,0},{1,17},{17,33},{33,49},{49,1},{2,18}... | collective-permute-start | bytes 1769480 | tf_op jit(solution)/shard_map/ppermute | solution.py:302
  54.6 4.4 %collective-permute-start.10 = (bf16[8,48,768]{2,1,0:T(8,128)(2,1)S(1)}, bf16[8,48,768]{2,1,0:T(8,128)(2,1)S(1)}, u32[]{:S(2)}, u32[]{:S(2)}) collective-permute-start(bf16[8,48,768]{2,1,0:T(8,128)(2,1)S(1)} %all-to-all-done.one), channel_id=1, source_target_pairs={{0,32},{16,48},{32,0},{48,16},{1,33},{17,49},{33,1},{49,17},{2,34}... | collective-permute-start | bytes 1769480 | tf_op jit(solution)/shard_map/ppermute | solution.py:302
  59.0 2.2 %collective-permute-start.9 = (bf16[8,48,768]{2,1,0:T(8,128)(2,1)S(1)}, bf16[8,48,768]{2,1,0:T(8,128)(2,1)}, u32[]{:S(2)}, u32[]{:S(2)}) collective-permute-start(bf16[8,48,768]{2,1,0:T(8,128)(2,1)S(1)} %all-to-all-done.one), channel_id=1, source_target_pairs={{0,48},{16,0},{32,16},{48,32},{1,49},{17,1},{33,17},{49,33},{2,50}... | collective-permute-start | bytes 1769480 | tf_op jit(solution)/shard_map/ppermute | solution.py:302
  61.3 0.0 collective-permute-done.7
  61.3 0.0 all-to-all-done.1.chunks
  61.3 2.0 %shard_map.97 = (bf16[128,192]{1,0:T(8,128)(2,1)}, bf16[128,192]{1,0:T(8,128)(2,1)}) custom-call(s32[3]{0:T(128)} %pad_add_fusion.place, bf16[8,144,128]{2,1,0:T(8,128)(2,1)} %all-to-all-done.1.chunks), custom_call_target="tpu_custom_call" | custom-call | tf_op jit(solution)/shard_map/pallas_call | solution.py:144
  63.3 3.9 %collective-permute-start.8 = (bf16[128,192]{1,0:T(8,128)(2,1)}, bf16[128,192]{1,0:T(8,128)(2,1)}, u32[]{:S(2)}, u32[]{:S(2)}) collective-permute-start(bf16[128,192]{1,0:T(8,128)(2,1)} %get-tuple-element.50), channel_id=1, source_target_pairs={{0,8},{8,0},{1,9},{9,1},{2,10},{10,2},{3,11},{11,3},{4,12},{12,4},... | collective-permute-start | bytes 147464 | tf_op jit(solution)/shard_map/ppermute | solution.py:32
  67.3 2.5 %collective-permute-done.8 = bf16[128,192]{1,0:T(8,128)(2,1)} collective-permute-done((bf16[128,192]{1,0:T(8,128)(2,1)}, bf16[128,192]{1,0:T(8,128)(2,1)}, u32[]{:S(2)}, u32[]{:S(2)}) %collective-permute-start.8) | collective-permute-done | bytes 49184 | tf_op jit(solution)/shard_map/ppermute | solution.py:32
  69.8 1.0 pad_maximum_fusion.2
  70.8 19.4 %all-gather = bf16[512,384]{1,0:T(8,128)(2,1)S(1)} all-gather(bf16[128,384]{1,0:T(8,128)(2,1)S(1)} %pad_maximum_fusion.2), channel_id=2, replica_groups=mesh['h'=2,'y'=4,'x'=4,'z'=2,'w'=4,'c'=2] {'w'}, dimensions={0}, use_global_device_ids=true | all-gather | bytes 491520 | tf_op jit(solution)/shard_map/all_gather | solution.py:308
  90.1 2.4 %all-gather.1 = bf16[4,256,384]{2,1,0:T(8,128)(2,1)S(1)} all-gather(bf16[4,128,384]{2,1,0:T(8,128)(2,1)S(1)} %bitcast.37), channel_id=3, replica_groups=mesh['h'=2,'y'=4,'x'=4,'z'=2,'w'=4,'c'=2] {'c'}, dimensions={1}, use_global_device_ids=true | all-gather | bytes 1179648 | tf_op jit(solution)/shard_map/all_gather | solution.py:309
  92.5 0.0 collective-permute-done.11.four
  92.5 0.0 collective-permute-done.10.three
  92.5 0.0 collective-permute-done.9.two
  92.5 0.0 copy-done.1
  92.5 0.0 copy-done.3
  92.5 0.0 copy-start.4
  92.5 2.1 %shard_map.99 = (f32[256,768]{1,0:T(8,128)S(1)}, bf16[272,768]{1,0:T(8,128)(2,1)S(1)}) custom-call(bf16[8,128,384]{2,1,0:T(8,128)(2,1)S(1)} %bitcast.33, bf16[128,768]{1,0:T(8,128)(2,1)S(1)} %copy-done.1, f32[2,128]{1,0:T(2,128)S(1)} %copy-done.3, bf16[8,48,768]{2,1,0:T(8,128)(2,1)S(1)} %all-to-all-done.one, bf16[8,48,768]{2,1,0:T(8,128)(2,1)} %collective-permute-done.9.two, ...), custom_call_target="tpu_custom_call" | custom-call | flops 603979776 | bytes 2359296 | tf_op jit(solution)/shard_map/pallas_call | solution.py:184
  94.7 5.0 %collective-permute-start.12 = (bf16[272,768]{1,0:T(8,128)(2,1)S(1)}, bf16[272,768]{1,0:T(8,128)(2,1)S(1)}, u32[]{:S(2)}, u32[]{:S(2)}) collective-permute-start(bf16[272,768]{1,0:T(8,128)(2,1)S(1)} %get-tuple-element.56), channel_id=1, source_target_pairs={{0,8},{8,0},{1,9},{9,1},{2,10},{10,2},{3,11},{11,3},{4,12},{12,4},... | collective-permute-start | bytes 1253384 | tf_op jit(solution)/shard_map/ppermute | solution.py:32
  99.6 0.0 copy-done
  99.6 0.0 copy-done.4
  99.6 0.6 fusion.pred
  100.3 1.0 dynamic-slice_bitcast_fusion
  101.3 0.1 maximum_bitcast_fusion
  101.4 1.6 %fusion.1.pred_far = f32[256,768]{1,0:T(8,128)S(1)} fusion(bf16[256,1024]{0,1:T(8,128)(2,1)} %collective-permute-done.7, bf16[1024,768]{1,0:T(8,128)(2,1)S(1)} %copy-done), kind=kOutput, calls=%fused_computation.14 | convolution fusion | flops 402653184 | bytes 2883584 | tf_op jit(solution)/shard_map/dot_general | solution.py:315
  103.0 6.5 %collective-permute-done.12.arrived = bf16[272,768]{1,0:T(8,128)(2,1)S(1)} collective-permute-done((bf16[272,768]{1,0:T(8,128)(2,1)S(1)}, bf16[272,768]{1,0:T(8,128)(2,1)S(1)}, u32[]{:S(2)}, u32[]{:S(2)}) %collective-permute-start.12) | collective-permute-done | bytes 417824 | tf_op jit(solution)/shard_map/ppermute | solution.py:32
  109.6 0.3 shard_map.100
  109.8 12.1 %all_to_all.25.stats = f32[8,4,128]{2,1,0:T(4,128)S(1)} all-to-all(f32[8,4,128]{2,1,0:T(4,128)S(1)} %get-tuple-element.61), channel_id=1, replica_groups=mesh['h'=2,'y'=4,'x'=4,'z'=2,'w'=4,'c'=2] {'w','c'}, dimensions={0} | all-to-all | bytes 32768 | tf_op jit(solution)/shard_map/all_to_all | solution.py:328
  121.9 1.4 shard_map.101
  123.3 15.4 %all_to_all.26 = bf16[4,128,768]{2,1,0:T(8,128)(2,1)S(1)} all-to-all(bf16[4,128,768]{2,1,0:T(8,128)(2,1)S(1)} %bitcast.35), channel_id=1, replica_groups=mesh['h'=2,'y'=4,'x'=4,'z'=2,'w'=4,'c'=2] {'x'}, dimensions={0} | all-to-all | bytes 1572864 | tf_op jit(solution)/shard_map/all_to_all | solution.py:331
  138.7 0.1 reduce_sum.21
  138.8 15.7 %all_to_all.27 = bf16[8,16,768]{2,1,0:T(8,128)(2,1)S(1)} all-to-all(bf16[8,16,768]{2,1,0:T(8,128)(2,1)S(1)} %bitcast.38), channel_id=1, replica_groups=mesh['h'=2,'y'=4,'x'=4,'z'=2,'w'=4,'c'=2] {'h','y'}, dimensions={0} | all-to-all | bytes 393216 | tf_op jit(solution)/shard_map/all_to_all | solution.py:333
  154.5 0.6 broadcast_multiply_fusion
  (10 shorter events, 0.2 us)
Async XLA Ops:
  0.6 99.0 %copy-start = (bf16[1024,768]{1,0:T(8,128)(2,1)S(1)}, bf16[1024,768]{1,0:T(8,128)(2,1)}, u32[]{:S(2)}) copy-start(bf16[1024,768]{1,0:T(8,128)(2,1)} %param.14) | copy-start | bytes 4718596
  3.3 7.9 %collective-permute-start = (bf16[3,128,128]{2,1,0:T(8,128)(2,1)}, bf16[3,128,128]{2,1,0:T(8,128)(2,1)S(1)}, u32[]{:S(2)}, u32[]{:S(2)}) collective-permute-start(bf16[3,128,128]{2,1,0:T(8,128)(2,1)} %get-tuple-element.36), channel_id=1, source_target_pairs={{0,64},{64,0},{192,128},{1,65},{65,1},{193,129},{2,66},{66,2},{194... | collective-permute-start | bytes 294920 | tf_op jit(solution)/shard_map/ppermute | solution.py:284
  6.8 12.9 %collective-permute-start.1 = (bf16[3,128,128]{2,1,0:T(8,128)(2,1)}, bf16[3,128,128]{2,1,0:T(8,128)(2,1)S(1)}, u32[]{:S(2)}, u32[]{:S(2)}) collective-permute-start(bf16[3,128,128]{2,1,0:T(8,128)(2,1)} %get-tuple-element.39), channel_id=1, source_target_pairs={{0,128},{128,0},{192,64},{1,129},{129,1},{193,65},{2,130},{130,2},... | collective-permute-start | bytes 294920 | tf_op jit(solution)/shard_map/ppermute | solution.py:284
  9.1 10.7 %collective-permute-start.2 = (bf16[3,128,128]{2,1,0:T(8,128)(2,1)}, bf16[3,128,128]{2,1,0:T(8,128)(2,1)S(1)}, u32[]{:S(2)}, u32[]{:S(2)}) collective-permute-start(bf16[3,128,128]{2,1,0:T(8,128)(2,1)} %get-tuple-element.40), channel_id=1, source_target_pairs={{64,128},{128,64},{192,0},{65,129},{129,65},{193,1},{66,130},{130,... | collective-permute-start | bytes 294920 | tf_op jit(solution)/shard_map/ppermute | solution.py:284
  11.3 28.8 %copy-start.2 = (s32[3]{0:T(128)S(1)}, s32[3]{0:T(128)}, u32[]{:S(2)}) copy-start(s32[3]{0:T(128)} %pad_add_fusion.place) | copy-start | bytes 40
  11.3 28.8 %all-to-all-start = ((bf16[8,48,768]{2,1,0:T(8,128)(2,1)}), bf16[8,48,768]{2,1,0:T(8,128)(2,1)S(1)}, u32[]{:S(2)}, u32[]{:S(2)}) async-start(bf16[8,48,768]{2,1,0:T(8,128)(2,1)} %get-tuple-element.41), calls=%async_computation | async-start | bytes 1179648 | tf_op jit(solution)/shard_map/all_to_all | solution.py:290
  19.8 20.2 %collective-permute-start.5 = (bf16[4,2,128,128]{3,2,1,0:T(8,128)(2,1)S(1)}, bf16[4,2,128,128]{3,2,1,0:T(8,128)(2,1)S(1)}, u32[]{:S(2)}, u32[]{:S(2)}) collective-permute-start(bf16[4,2,128,128]{3,2,1,0:T(8,128)(2,1)S(1)} %pad_maximum_fusion.kv0), channel_id=1, source_target_pairs={{0,48},{16,0},{32,16},{48,32},{1,49},{17,1},{33,17},{49,33},{2,50}... | collective-permute-start | bytes 786440 | tf_op jit(solution)/shard_map/ppermute | solution.py:292
  23.6 16.4 %collective-permute-start.4 = (bf16[4,2,128,128]{3,2,1,0:T(8,128)(2,1)S(1)}, bf16[4,2,128,128]{3,2,1,0:T(8,128)(2,1)S(1)}, u32[]{:S(2)}, u32[]{:S(2)}) collective-permute-start(bf16[4,2,128,128]{3,2,1,0:T(8,128)(2,1)S(1)} %pad_maximum_fusion.kv0), channel_id=1, source_target_pairs={{0,16},{16,32},{32,48},{48,0},{1,17},{17,33},{33,49},{49,1},{2,18}... | collective-permute-start | bytes 786440 | tf_op jit(solution)/shard_map/ppermute | solution.py:292
  25.7 14.4 %collective-permute-start.3 = (bf16[4,2,128,128]{3,2,1,0:T(8,128)(2,1)S(1)}, bf16[4,2,128,128]{3,2,1,0:T(8,128)(2,1)S(1)}, u32[]{:S(2)}, u32[]{:S(2)}) collective-permute-start(bf16[4,2,128,128]{3,2,1,0:T(8,128)(2,1)S(1)} %pad_maximum_fusion.kv0), channel_id=1, source_target_pairs={{0,32},{16,48},{32,0},{48,16},{1,33},{17,49},{33,1},{49,17},{2,34}... | collective-permute-start | bytes 786440 | tf_op jit(solution)/shard_map/ppermute | solution.py:292
  31.8 8.3 %collective-permute-start.6 = (bf16[4,128,128]{2,1,0:T(8,128)(2,1)S(1)}, bf16[4,128,128]{2,1,0:T(8,128)(2,1)S(1)}, u32[]{:S(2)}, u32[]{:S(2)}) collective-permute-start(bf16[4,128,128]{2,1,0:T(8,128)(2,1)S(1)} %pad_maximum_fusion.1.q_own), channel_id=1, source_target_pairs={{0,8},{8,0},{1,9},{9,1},{2,10},{10,2},{3,11},{11,3},{4,12},{12,4},... | collective-permute-start | bytes 393224 | tf_op jit(solution)/shard_map/ppermute | solution.py:32
  38.1 23.2 %collective-permute-start.7 = (bf16[256,1024]{0,1:T(8,128)(2,1)}, bf16[256,1024]{0,1:T(8,128)(2,1)}, u32[]{:S(2)}, u32[]{:S(2)}) collective-permute-start(bf16[256,1024]{0,1:T(8,128)(2,1)} %copy.17), channel_id=1, source_target_pairs={{0,8},{8,0},{1,9},{9,1},{2,10},{10,2},{3,11},{11,3},{4,12},{12,4},... | collective-permute-start | bytes 1572872 | tf_op jit(solution)/shard_map/ppermute | solution.py:32
  44.8 16.5 %all-to-all-start.1 = ((bf16[8,144,128]{2,1,0:T(8,128)(2,1)}), bf16[8,144,128]{2,1,0:T(8,128)(2,1)}, u32[]{:S(2)}, u32[]{:S(2)}) async-start(bf16[8,144,128]{2,1,0:T(8,128)(2,1)} %shard_map.96), calls=%async_computation.1 | async-start | bytes 589824 | tf_op jit(solution)/shard_map/all_to_all | solution.py:304
  52.6 39.9 %copy-start.1 = (bf16[128,768]{1,0:T(8,128)(2,1)S(1)}, bf16[128,768]{1,0:T(8,128)(2,1)}, u32[]{:S(2)}) copy-start(bf16[128,768]{1,0:T(8,128)(2,1)} %residual.1) | copy-start | bytes 589828
  52.6 39.9 %copy-start.3 = (f32[2,128]{1,0:T(2,128)S(1)}, f32[2,128]{1,0:T(2,128)}, u32[]{:S(2)}) copy-start(f32[2,128]{1,0:T(2,128)} %shard_map.98.mask) | copy-start | bytes 3076
  52.6 39.9 %collective-permute-start.11 = (bf16[8,48,768]{2,1,0:T(8,128)(2,1)S(1)}, bf16[8,48,768]{2,1,0:T(8,128)(2,1)S(1)}, u32[]{:S(2)}, u32[]{:S(2)}) collective-permute-start(bf16[8,48,768]{2,1,0:T(8,128)(2,1)S(1)} %all-to-all-done.one), channel_id=1, source_target_pairs={{0,16},{16,32},{32,48},{48,0},{1,17},{17,33},{33,49},{49,1},{2,18}... | collective-permute-start | bytes 1769480 | tf_op jit(solution)/shard_map/ppermute | solution.py:302
  54.6 37.9 %collective-permute-start.10 = (bf16[8,48,768]{2,1,0:T(8,128)(2,1)S(1)}, bf16[8,48,768]{2,1,0:T(8,128)(2,1)S(1)}, u32[]{:S(2)}, u32[]{:S(2)}) collective-permute-start(bf16[8,48,768]{2,1,0:T(8,128)(2,1)S(1)} %all-to-all-done.one), channel_id=1, source_target_pairs={{0,32},{16,48},{32,0},{48,16},{1,33},{17,49},{33,1},{49,17},{2,34}... | collective-permute-start | bytes 1769480 | tf_op jit(solution)/shard_map/ppermute | solution.py:302
  59.0 33.5 %collective-permute-start.9 = (bf16[8,48,768]{2,1,0:T(8,128)(2,1)S(1)}, bf16[8,48,768]{2,1,0:T(8,128)(2,1)}, u32[]{:S(2)}, u32[]{:S(2)}) collective-permute-start(bf16[8,48,768]{2,1,0:T(8,128)(2,1)S(1)} %all-to-all-done.one), channel_id=1, source_target_pairs={{0,48},{16,0},{32,16},{48,32},{1,49},{17,1},{33,17},{49,33},{2,50}... | collective-permute-start | bytes 1769480 | tf_op jit(solution)/shard_map/ppermute | solution.py:302
  63.3 6.5 %collective-permute-start.8 = (bf16[128,192]{1,0:T(8,128)(2,1)}, bf16[128,192]{1,0:T(8,128)(2,1)}, u32[]{:S(2)}, u32[]{:S(2)}) collective-permute-start(bf16[128,192]{1,0:T(8,128)(2,1)} %get-tuple-element.50), channel_id=1, source_target_pairs={{0,8},{8,0},{1,9},{9,1},{2,10},{10,2},{3,11},{11,3},{4,12},{12,4},... | collective-permute-start | bytes 147464 | tf_op jit(solution)/shard_map/ppermute | solution.py:32
  92.5 7.1 %copy-start.4 = (bf16[256,1024]{0,1:T(8,128)(2,1)S(1)}, bf16[256,1024]{0,1:T(8,128)(2,1)}, u32[]{:S(2)}) copy-start(bf16[256,1024]{0,1:T(8,128)(2,1)} %copy.17) | copy-start | bytes 1572868
  94.7 14.9 %collective-permute-start.12 = (bf16[272,768]{1,0:T(8,128)(2,1)S(1)}, bf16[272,768]{1,0:T(8,128)(2,1)S(1)}, u32[]{:S(2)}, u32[]{:S(2)}) collective-permute-start(bf16[272,768]{1,0:T(8,128)(2,1)S(1)} %get-tuple-element.56), channel_id=1, source_target_pairs={{0,8},{8,0},{1,9},{9,1},{2,10},{10,2},{3,11},{11,3},{4,12},{12,4},... | collective-permute-start | bytes 1253384 | tf_op jit(solution)/shard_map/ppermute | solution.py:32
